TPU v7x, 256 devices: a whole 4x4x8 slice. The times are simulated.
256 devices in a mesh: section: 16 (over x, z_hi), expert: 16 (over z_lo, y, core).
Axes of the slice: x: 4, y: 4, z: 8 (z_hi: 4, z_lo: 2; z = z_hi * 2 + z_lo), core: 2. Of those that a mesh axis runs over, the one named last changes fastest.
Arguments:
- entering: bfloat16 [2, 2, 512, 3584], P(None, None, 'expert'), may hold values from -6 to 6
- norm_gain: float32 [16, 3584], P('section'), may hold values from 0.5 to 1.5
- w_gate: bfloat16 [16, 3584, 8192], P('section', None, 'expert'), may hold values from -0.09375 to 0.09375
- w_up: bfloat16 [16, 3584, 8192], P('section', None, 'expert'), may hold values from -0.09375 to 0.09375
- w_down: bfloat16 [16, 8192, 3584], P('section', 'expert'), may hold values from -0.1875 to 0.1875
- route_ids: int32 [2, 2, 16, 512, 8], P(None, None, 'section', 'expert'), may hold values from 0 to 255, as said below
- route_scores: float32 [2, 2, 16, 512, 8], P(None, None, 'section', 'expert'), may hold values from 0.05 to 1
Outputs:
- leaving: bfloat16 [2, 2, 512, 3584], P(None, None, 'expert', 'section')
Inputs may be any that keep to these rules, and one draw needn't show every extreme that they name: `route_ids`: A token's 8 ids are distinct. In every block of 32 tokens (one direction, micro-batch and layer), at most 2 tokens name any one expert below 8, and in every such block exactly 2 tokens name one of them.
All inputs are finite; a program needn't handle non-finite values.
Results may differ from a plain program's by a relative error of at most 0.0072.
Values may be sent and summed in bfloat16 or wider, within the bound.
A program may use at most 64 MiB of HBM per device.

v0:
```python
import jax
import jax.numpy as jnp
from jax import lax
from jax.sharding import PartitionSpec as P

GROUP = 2
CAP = 2


norm_eps = 1e-06
route_scale = 2.5


def from_behind(value, axis, steps):
    count = lax.axis_size(axis)
    initial, last = (max(0, -steps), min(count, count - steps))
    return lax.ppermute(value, axis, [(source, source + steps) for source in range(initial, last)])


def in_one_piece(arrays, axis, dim, along):
    widths = [a.shape[along] for a in arrays]
    both = jnp.concatenate(arrays, axis=along)
    out = lax.psum_scatter(both, axis, scatter_dimension=dim, tiled=True)
    return tuple(jnp.split(out, [sum(widths[:k]) for k in range(1, len(widths))], axis=along))


def on_device(entering, norm_gain, w_gate, w_up, w_down, route_ids, route_scores):
    sections = lax.axis_size("section")
    spread = lax.axis_size("expert")
    section = lax.axis_index("section")
    window = spread // GROUP
    micro = entering.shape[1]
    tokens = entering.shape[2]
    width = entering.shape[3]
    gain = norm_gain[0]
    wgate = w_gate[0]
    wup = w_up[0]
    wdown = w_down[0]
    steps = micro + sections - 1
    earlier = (jnp.arange(tokens)[:, None] > jnp.arange(tokens)[None, :]).astype(jnp.float32)
    expert_iota = jnp.arange(window, dtype=jnp.int32)
    slot_iota = jnp.arange(CAP, dtype=jnp.float32)

    def prepare(x, ids, scores):
        xf = x.astype(jnp.float32)
        normed = (
            xf * lax.rsqrt(jnp.mean(xf * xf, axis=-1, keepdims=True) + norm_eps) * gain
        ).astype(jnp.bfloat16)
        weights = route_scale * scores / jnp.sum(scores, axis=-1, keepdims=True)
        hit = (ids[:, :, None] == expert_iota).astype(jnp.float32)
        count = jnp.sum(hit, axis=1)
        share = jnp.sum(weights[:, :, None] * hit, axis=1)
        before = jnp.dot(earlier, count, precision=lax.Precision.HIGHEST)
        place = count.T[:, None, :] * (before.T[:, None, :] == slot_iota[None, :, None]).astype(
            jnp.float32
        )
        blocks = jnp.einsum(
            "ect,td->ecd", place.astype(jnp.bfloat16), normed, preferred_element_type=jnp.float32
        ).astype(jnp.bfloat16)
        sending = jnp.repeat(blocks, GROUP, axis=0)
        comb = place * share.T[:, None, :]
        return (sending, comb)

    def expert_rows(received):
        count = received.shape[1]
        rows = received.reshape(-1, width)
        gate = jnp.dot(rows, wgate, preferred_element_type=jnp.float32)
        up = jnp.dot(rows, wup, preferred_element_type=jnp.float32)
        act = (jax.nn.silu(gate) * up).astype(jnp.bfloat16)
        part = (
            jnp.dot(act, wdown, preferred_element_type=jnp.float32)
            .astype(jnp.bfloat16)
            .reshape(spread, count, width)
        )
        back = lax.all_to_all(part, "expert", split_axis=0, concat_axis=0, tiled=True)
        return jnp.sum(back.astype(jnp.float32).reshape(window, GROUP, count, width), axis=1)

    def finish(x, comb, result):
        added = jnp.einsum("ect,ecd->td", comb, result, precision=lax.Precision.HIGHEST)
        return (x.astype(jnp.float32) + added).astype(jnp.bfloat16)

    def advance(step, carry):
        prev_f, prev_r, done_f, done_r = carry
        from_f = from_behind(prev_f, "section", 1)
        from_r = from_behind(prev_r, "section", -1)
        feed_index = jnp.clip(step, 0, micro - 1)
        feed_f = lax.dynamic_index_in_dim(entering[0], feed_index, 0, keepdims=False)
        feed_r = lax.dynamic_index_in_dim(entering[1], feed_index, 0, keepdims=False)
        x_f = jnp.where(section == 0, feed_f, from_f)
        x_r = jnp.where(section == sections - 1, feed_r, from_r)
        index_f = jnp.clip(step - section, 0, micro - 1)
        index_r = jnp.clip(step - (sections - 1 - section), 0, micro - 1)
        ids_f = lax.dynamic_index_in_dim(route_ids[0, :, 0], index_f, 0, keepdims=False)
        ids_r = lax.dynamic_index_in_dim(route_ids[1, :, 0], index_r, 0, keepdims=False)
        sc_f = lax.dynamic_index_in_dim(route_scores[0, :, 0], index_f, 0, keepdims=False)
        sc_r = lax.dynamic_index_in_dim(route_scores[1, :, 0], index_r, 0, keepdims=False)
        send_f, comb_f = prepare(x_f, ids_f, sc_f)
        send_r, comb_r = prepare(x_r, ids_r, sc_r)
        both = jnp.concatenate([send_f, send_r], axis=1)
        result = expert_rows(
            lax.all_to_all(both, "expert", split_axis=0, concat_axis=0, tiled=True)
        )
        result_f = result[:, :CAP]
        result_r = result[:, CAP:]
        out_f = finish(x_f, comb_f, result_f)
        out_r = finish(x_r, comb_r, result_r)
        leave_index = step - (sections - 1)
        safe_index = jnp.clip(leave_index, 0, micro - 1)
        valid = leave_index >= 0
        done_f = jnp.where(
            valid & (section == sections - 1),
            lax.dynamic_update_index_in_dim(done_f, out_f, safe_index, 0),
            done_f,
        )
        done_r = jnp.where(
            valid & (section == 0),
            lax.dynamic_update_index_in_dim(done_r, out_r, safe_index, 0),
            done_r,
        )
        return (out_f, out_r, done_f, done_r)

    blank = jnp.zeros((tokens, width), jnp.bfloat16)
    store = jnp.zeros((micro, tokens, width), jnp.bfloat16)
    unused_f, unused_r, done_f, done_r = lax.fori_loop(
        0, steps, advance, (blank, blank, store, store)
    )
    term_f = jnp.where(section == sections - 1, done_f.astype(jnp.float32), 0.0)
    term_r = jnp.where(section == 0, done_r.astype(jnp.float32), 0.0)
    final_f, final_r = tuple(
        (
            part.astype(jnp.float32)
            for part in in_one_piece(
                (term_f.astype(jnp.bfloat16), term_r.astype(jnp.bfloat16)), "section", 2, 0
            )
        )
    )
    return jnp.stack([final_f, final_r]).astype(jnp.bfloat16)


def solution(mesh):
    return jax.shard_map(
        on_device,
        mesh=mesh,
        in_specs=(
            P(None, None, "expert", None),
            P("section", None),
            P("section", None, "expert"),
            P("section", None, "expert"),
            P("section", "expert", None),
            P(None, None, "section", "expert", None),
            P(None, None, "section", "expert", None),
        ),
        out_specs=P(None, None, "expert", "section"),
        check_vma=False,
    )
```

profile of v0, /device:TPU:61, one launch (start us, length us, event | category | flops | bytes accessed | tf_op | source)
XLA Modules:
  0.0 1091.7 jit_solution(12878512999433918402)
XLA Ops:
  6.6 983.9 %while.23 = (s32[]{:T(128)}, bf16[32,3584]{1,0:T(8,128)(2,1)S(1)}, bf16[32,3584]{1,0:T(8,128)(2,1)S(1)}, bf16[2,32,3584]{2,1,0:T(8,128)(2,1)S(1)}, bf16[2,32,358...) while((s32[]{:T(128)}, bf16[32,3584]{1,0:T(8,128)(2,1)S(1)}, ...), condition=%wide.region_10.11_spmd.clone.clone, body=%wide.region_0.10_spmd.clone.clone.sunk | while | flops 761034240 | bytes 29749232 | solution.py:124
  25.9 16.1 %all_to_all.30 = bf16[16,4,3584]{2,1,0:T(4,128)(2,1)S(1)} all-to-all(bf16[16,4,3584]{2,1,0:T(4,128)(2,1)S(1)} %pad_maximum_fusion.4), channel_id=1, replica_groups=mesh['section'=16,'expert'=16] {'expert'}, dimensions={0} | all-to-all | bytes 917504 | tf_op jit(solution)/shard_map/while/body/eval_jaxpr/all_to_all | solution.py:101
  56.8 7.2 all-to-all-done.1
  82.7 18.6 %all_to_all.30 = bf16[16,4,3584]{2,1,0:T(4,128)(2,1)S(1)} all-to-all(bf16[16,4,3584]{2,1,0:T(4,128)(2,1)S(1)} %pad_maximum_fusion.4), channel_id=1, replica_groups=mesh['section'=16,'expert'=16] {'expert'}, dimensions={0} | all-to-all | bytes 917504 | tf_op jit(solution)/shard_map/while/body/eval_jaxpr/all_to_all | solution.py:101
  116.1 7.2 all-to-all-done.1
  141.1 16.8 %all_to_all.30 = bf16[16,4,3584]{2,1,0:T(4,128)(2,1)S(1)} all-to-all(bf16[16,4,3584]{2,1,0:T(4,128)(2,1)S(1)} %pad_maximum_fusion.4), channel_id=1, replica_groups=mesh['section'=16,'expert'=16] {'expert'}, dimensions={0} | all-to-all | bytes 917504 | tf_op jit(solution)/shard_map/while/body/eval_jaxpr/all_to_all | solution.py:101
  200.6 15.3 %all_to_all.30 = bf16[16,4,3584]{2,1,0:T(4,128)(2,1)S(1)} all-to-all(bf16[16,4,3584]{2,1,0:T(4,128)(2,1)S(1)} %pad_maximum_fusion.4), channel_id=1, replica_groups=mesh['section'=16,'expert'=16] {'expert'}, dimensions={0} | all-to-all | bytes 917504 | tf_op jit(solution)/shard_map/while/body/eval_jaxpr/all_to_all | solution.py:101
  257.1 17.4 %all_to_all.30 = bf16[16,4,3584]{2,1,0:T(4,128)(2,1)S(1)} all-to-all(bf16[16,4,3584]{2,1,0:T(4,128)(2,1)S(1)} %pad_maximum_fusion.4), channel_id=1, replica_groups=mesh['section'=16,'expert'=16] {'expert'}, dimensions={0} | all-to-all | bytes 917504 | tf_op jit(solution)/shard_map/while/body/eval_jaxpr/all_to_all | solution.py:101
  314.6 18.6 %all_to_all.30 = bf16[16,4,3584]{2,1,0:T(4,128)(2,1)S(1)} all-to-all(bf16[16,4,3584]{2,1,0:T(4,128)(2,1)S(1)} %pad_maximum_fusion.4), channel_id=1, replica_groups=mesh['section'=16,'expert'=16] {'expert'}, dimensions={0} | all-to-all | bytes 917504 | tf_op jit(solution)/shard_map/while/body/eval_jaxpr/all_to_all | solution.py:101
  372.2 18.3 %all_to_all.30 = bf16[16,4,3584]{2,1,0:T(4,128)(2,1)S(1)} all-to-all(bf16[16,4,3584]{2,1,0:T(4,128)(2,1)S(1)} %pad_maximum_fusion.4), channel_id=1, replica_groups=mesh['section'=16,'expert'=16] {'expert'}, dimensions={0} | all-to-all | bytes 917504 | tf_op jit(solution)/shard_map/while/body/eval_jaxpr/all_to_all | solution.py:101
  431.4 16.8 %all_to_all.30 = bf16[16,4,3584]{2,1,0:T(4,128)(2,1)S(1)} all-to-all(bf16[16,4,3584]{2,1,0:T(4,128)(2,1)S(1)} %pad_maximum_fusion.4), channel_id=1, replica_groups=mesh['section'=16,'expert'=16] {'expert'}, dimensions={0} | all-to-all | bytes 917504 | tf_op jit(solution)/shard_map/while/body/eval_jaxpr/all_to_all | solution.py:101
  487.3 18.2 %all_to_all.30 = bf16[16,4,3584]{2,1,0:T(4,128)(2,1)S(1)} all-to-all(bf16[16,4,3584]{2,1,0:T(4,128)(2,1)S(1)} %pad_maximum_fusion.4), channel_id=1, replica_groups=mesh['section'=16,'expert'=16] {'expert'}, dimensions={0} | all-to-all | bytes 917504 | tf_op jit(solution)/shard_map/while/body/eval_jaxpr/all_to_all | solution.py:101
  520.3 7.2 all-to-all-done.1
  546.5 17.0 %all_to_all.30 = bf16[16,4,3584]{2,1,0:T(4,128)(2,1)S(1)} all-to-all(bf16[16,4,3584]{2,1,0:T(4,128)(2,1)S(1)} %pad_maximum_fusion.4), channel_id=1, replica_groups=mesh['section'=16,'expert'=16] {'expert'}, dimensions={0} | all-to-all | bytes 917504 | tf_op jit(solution)/shard_map/while/body/eval_jaxpr/all_to_all | solution.py:101
  602.5 18.3 %all_to_all.30 = bf16[16,4,3584]{2,1,0:T(4,128)(2,1)S(1)} all-to-all(bf16[16,4,3584]{2,1,0:T(4,128)(2,1)S(1)} %pad_maximum_fusion.4), channel_id=1, replica_groups=mesh['section'=16,'expert'=16] {'expert'}, dimensions={0} | all-to-all | bytes 917504 | tf_op jit(solution)/shard_map/while/body/eval_jaxpr/all_to_all | solution.py:101
  635.7 7.2 all-to-all-done.1
  661.5 17.3 %all_to_all.30 = bf16[16,4,3584]{2,1,0:T(4,128)(2,1)S(1)} all-to-all(bf16[16,4,3584]{2,1,0:T(4,128)(2,1)S(1)} %pad_maximum_fusion.4), channel_id=1, replica_groups=mesh['section'=16,'expert'=16] {'expert'}, dimensions={0} | all-to-all | bytes 917504 | tf_op jit(solution)/shard_map/while/body/eval_jaxpr/all_to_all | solution.py:101
  717.9 18.3 %all_to_all.30 = bf16[16,4,3584]{2,1,0:T(4,128)(2,1)S(1)} all-to-all(bf16[16,4,3584]{2,1,0:T(4,128)(2,1)S(1)} %pad_maximum_fusion.4), channel_id=1, replica_groups=mesh['section'=16,'expert'=16] {'expert'}, dimensions={0} | all-to-all | bytes 917504 | tf_op jit(solution)/shard_map/while/body/eval_jaxpr/all_to_all | solution.py:101
  775.7 18.4 %all_to_all.30 = bf16[16,4,3584]{2,1,0:T(4,128)(2,1)S(1)} all-to-all(bf16[16,4,3584]{2,1,0:T(4,128)(2,1)S(1)} %pad_maximum_fusion.4), channel_id=1, replica_groups=mesh['section'=16,'expert'=16] {'expert'}, dimensions={0} | all-to-all | bytes 917504 | tf_op jit(solution)/shard_map/while/body/eval_jaxpr/all_to_all | solution.py:101
  809.0 7.2 all-to-all-done.1
  833.2 18.3 %all_to_all.30 = bf16[16,4,3584]{2,1,0:T(4,128)(2,1)S(1)} all-to-all(bf16[16,4,3584]{2,1,0:T(4,128)(2,1)S(1)} %pad_maximum_fusion.4), channel_id=1, replica_groups=mesh['section'=16,'expert'=16] {'expert'}, dimensions={0} | all-to-all | bytes 917504 | tf_op jit(solution)/shard_map/while/body/eval_jaxpr/all_to_all | solution.py:101
  891.1 18.4 %all_to_all.30 = bf16[16,4,3584]{2,1,0:T(4,128)(2,1)S(1)} all-to-all(bf16[16,4,3584]{2,1,0:T(4,128)(2,1)S(1)} %pad_maximum_fusion.4), channel_id=1, replica_groups=mesh['section'=16,'expert'=16] {'expert'}, dimensions={0} | all-to-all | bytes 917504 | tf_op jit(solution)/shard_map/while/body/eval_jaxpr/all_to_all | solution.py:101
  948.5 18.3 %all_to_all.30 = bf16[16,4,3584]{2,1,0:T(4,128)(2,1)S(1)} all-to-all(bf16[16,4,3584]{2,1,0:T(4,128)(2,1)S(1)} %pad_maximum_fusion.4), channel_id=1, replica_groups=mesh['section'=16,'expert'=16] {'expert'}, dimensions={0} | all-to-all | bytes 917504 | tf_op jit(solution)/shard_map/while/body/eval_jaxpr/all_to_all | solution.py:101
  1000.2 82.6 %reduce-scatter.4.cloned.1.call-done = bf16[224,128]{1,0:T(8,128)(2,1)} async-done(((bf16[3584,128]{1,0:T(8,128)(2,1)}), bf16[224,128]{1,0:T(8,128)(2,1)}) %reduce-scatter.4.cloned.1.call-update) | async-done | bytes 57360
  (673 shorter events, 655.5 us)
Async XLA Ops:
  6.5 1076.3 %reduce-scatter.4.cloned.1.call-start = ((), (), s32[]{:S(2)}) async-start(), calls=%async_computation.3 | async-start | bytes 974848
  6.7 17.6 %collective-permute-start.1 = (bf16[32,3584]{1,0:T(8,128)(2,1)S(1)}, bf16[32,3584]{1,0:T(8,128)(2,1)S(1)}, u32[]{:S(2)}, u32[]{:S(2)}) collective-permute-start(bf16[32,3584]{1,0:T(8,128)(2,1)S(1)} %broadcast_select_fusion.5), channel_id=1, source_target_pairs={{0,16},{16,32},{32,48},{48,64},{64,80},{80,96},{96,112},{112,128},... | collective-permute-start | bytes 688136 | tf_op jit(solution)/shard_map/while/body/eval_jaxpr/ppermute | solution.py:17
  50.4 13.6 %all-to-all-start.1 = ((bf16[16,4,3584]{2,1,0:T(4,128)(2,1)}), bf16[16,4,3584]{2,1,0:T(4,128)(2,1)S(1)}, u32[]{:S(2)}, u32[]{:S(2)}) async-start(bf16[16,4,3584]{2,1,0:T(4,128)(2,1)} %reshape.179), calls=%async_computation.1 | async-start | bytes 917504 | tf_op jit(solution)/shard_map/while/body/eval_jaxpr/all_to_all | solution.py:75
  65.7 15.3 %collective-permute-start.1 = (bf16[32,3584]{1,0:T(8,128)(2,1)S(1)}, bf16[32,3584]{1,0:T(8,128)(2,1)S(1)}, u32[]{:S(2)}, u32[]{:S(2)}) collective-permute-start(bf16[32,3584]{1,0:T(8,128)(2,1)S(1)} %broadcast_select_fusion.5), channel_id=1, source_target_pairs={{0,16},{16,32},{32,48},{48,64},{64,80},{80,96},{96,112},{112,128},... | collective-permute-start | bytes 688136 | tf_op jit(solution)/shard_map/while/body/eval_jaxpr/ppermute | solution.py:17
  125.0 14.5 %collective-permute-start.1 = (bf16[32,3584]{1,0:T(8,128)(2,1)S(1)}, bf16[32,3584]{1,0:T(8,128)(2,1)S(1)}, u32[]{:S(2)}, u32[]{:S(2)}) collective-permute-start(bf16[32,3584]{1,0:T(8,128)(2,1)S(1)} %broadcast_select_fusion.5), channel_id=1, source_target_pairs={{0,16},{16,32},{32,48},{48,64},{64,80},{80,96},{96,112},{112,128},... | collective-permute-start | bytes 688136 | tf_op jit(solution)/shard_map/while/body/eval_jaxpr/ppermute | solution.py:17
  181.7 17.3 %collective-permute-start.1 = (bf16[32,3584]{1,0:T(8,128)(2,1)S(1)}, bf16[32,3584]{1,0:T(8,128)(2,1)S(1)}, u32[]{:S(2)}, u32[]{:S(2)}) collective-permute-start(bf16[32,3584]{1,0:T(8,128)(2,1)S(1)} %broadcast_select_fusion.5), channel_id=1, source_target_pairs={{0,16},{16,32},{32,48},{48,64},{64,80},{80,96},{96,112},{112,128},... | collective-permute-start | bytes 688136 | tf_op jit(solution)/shard_map/while/body/eval_jaxpr/ppermute | solution.py:17
  239.7 15.8 %collective-permute-start.1 = (bf16[32,3584]{1,0:T(8,128)(2,1)S(1)}, bf16[32,3584]{1,0:T(8,128)(2,1)S(1)}, u32[]{:S(2)}, u32[]{:S(2)}) collective-permute-start(bf16[32,3584]{1,0:T(8,128)(2,1)S(1)} %broadcast_select_fusion.5), channel_id=1, source_target_pairs={{0,16},{16,32},{32,48},{48,64},{64,80},{80,96},{96,112},{112,128},... | collective-permute-start | bytes 688136 | tf_op jit(solution)/shard_map/while/body/eval_jaxpr/ppermute | solution.py:17
  298.3 14.6 %collective-permute-start.1 = (bf16[32,3584]{1,0:T(8,128)(2,1)S(1)}, bf16[32,3584]{1,0:T(8,128)(2,1)S(1)}, u32[]{:S(2)}, u32[]{:S(2)}) collective-permute-start(bf16[32,3584]{1,0:T(8,128)(2,1)S(1)} %broadcast_select_fusion.5), channel_id=1, source_target_pairs={{0,16},{16,32},{32,48},{48,64},{64,80},{80,96},{96,112},{112,128},... | collective-permute-start | bytes 688136 | tf_op jit(solution)/shard_map/while/body/eval_jaxpr/ppermute | solution.py:17
  341.6 13.6 %all-to-all-start.1 = ((bf16[16,4,3584]{2,1,0:T(4,128)(2,1)}), bf16[16,4,3584]{2,1,0:T(4,128)(2,1)S(1)}, u32[]{:S(2)}, u32[]{:S(2)}) async-start(bf16[16,4,3584]{2,1,0:T(4,128)(2,1)} %reshape.179), calls=%async_computation.1 | async-start | bytes 917504 | tf_op jit(solution)/shard_map/while/body/eval_jaxpr/all_to_all | solution.py:75
  356.9 13.6 %collective-permute-start.1 = (bf16[32,3584]{1,0:T(8,128)(2,1)S(1)}, bf16[32,3584]{1,0:T(8,128)(2,1)S(1)}, u32[]{:S(2)}, u32[]{:S(2)}) collective-permute-start(bf16[32,3584]{1,0:T(8,128)(2,1)S(1)} %broadcast_select_fusion.5), channel_id=1, source_target_pairs={{0,16},{16,32},{32,48},{48,64},{64,80},{80,96},{96,112},{112,128},... | collective-permute-start | bytes 688136 | tf_op jit(solution)/shard_map/while/body/eval_jaxpr/ppermute | solution.py:17
  398.9 13.6 %all-to-all-start.1 = ((bf16[16,4,3584]{2,1,0:T(4,128)(2,1)}), bf16[16,4,3584]{2,1,0:T(4,128)(2,1)S(1)}, u32[]{:S(2)}, u32[]{:S(2)}) async-start(bf16[16,4,3584]{2,1,0:T(4,128)(2,1)} %reshape.179), calls=%async_computation.1 | async-start | bytes 917504 | tf_op jit(solution)/shard_map/while/body/eval_jaxpr/all_to_all | solution.py:75
  414.3 15.5 %collective-permute-start.1 = (bf16[32,3584]{1,0:T(8,128)(2,1)S(1)}, bf16[32,3584]{1,0:T(8,128)(2,1)S(1)}, u32[]{:S(2)}, u32[]{:S(2)}) collective-permute-start(bf16[32,3584]{1,0:T(8,128)(2,1)S(1)} %broadcast_select_fusion.5), channel_id=1, source_target_pairs={{0,16},{16,32},{32,48},{48,64},{64,80},{80,96},{96,112},{112,128},... | collective-permute-start | bytes 688136 | tf_op jit(solution)/shard_map/while/body/eval_jaxpr/ppermute | solution.py:17
  471.9 13.8 %collective-permute-start.1 = (bf16[32,3584]{1,0:T(8,128)(2,1)S(1)}, bf16[32,3584]{1,0:T(8,128)(2,1)S(1)}, u32[]{:S(2)}, u32[]{:S(2)}) collective-permute-start(bf16[32,3584]{1,0:T(8,128)(2,1)S(1)} %broadcast_select_fusion.5), channel_id=1, source_target_pairs={{0,16},{16,32},{32,48},{48,64},{64,80},{80,96},{96,112},{112,128},... | collective-permute-start | bytes 688136 | tf_op jit(solution)/shard_map/while/body/eval_jaxpr/ppermute | solution.py:17
  529.2 15.6 %collective-permute-start.1 = (bf16[32,3584]{1,0:T(8,128)(2,1)S(1)}, bf16[32,3584]{1,0:T(8,128)(2,1)S(1)}, u32[]{:S(2)}, u32[]{:S(2)}) collective-permute-start(bf16[32,3584]{1,0:T(8,128)(2,1)S(1)} %broadcast_select_fusion.5), channel_id=1, source_target_pairs={{0,16},{16,32},{32,48},{48,64},{64,80},{80,96},{96,112},{112,128},... | collective-permute-start | bytes 688136 | tf_op jit(solution)/shard_map/while/body/eval_jaxpr/ppermute | solution.py:17
  587.2 13.7 %collective-permute-start.1 = (bf16[32,3584]{1,0:T(8,128)(2,1)S(1)}, bf16[32,3584]{1,0:T(8,128)(2,1)S(1)}, u32[]{:S(2)}, u32[]{:S(2)}) collective-permute-start(bf16[32,3584]{1,0:T(8,128)(2,1)S(1)} %broadcast_select_fusion.5), channel_id=1, source_target_pairs={{0,16},{16,32},{32,48},{48,64},{64,80},{80,96},{96,112},{112,128},... | collective-permute-start | bytes 688136 | tf_op jit(solution)/shard_map/while/body/eval_jaxpr/ppermute | solution.py:17
  629.3 13.6 %all-to-all-start.1 = ((bf16[16,4,3584]{2,1,0:T(4,128)(2,1)}), bf16[16,4,3584]{2,1,0:T(4,128)(2,1)S(1)}, u32[]{:S(2)}, u32[]{:S(2)}) async-start(bf16[16,4,3584]{2,1,0:T(4,128)(2,1)} %reshape.179), calls=%async_computation.1 | async-start | bytes 917504 | tf_op jit(solution)/shard_map/while/body/eval_jaxpr/all_to_all | solution.py:75
  644.6 15.2 %collective-permute-start.1 = (bf16[32,3584]{1,0:T(8,128)(2,1)S(1)}, bf16[32,3584]{1,0:T(8,128)(2,1)S(1)}, u32[]{:S(2)}, u32[]{:S(2)}) collective-permute-start(bf16[32,3584]{1,0:T(8,128)(2,1)S(1)} %broadcast_select_fusion.5), channel_id=1, source_target_pairs={{0,16},{16,32},{32,48},{48,64},{64,80},{80,96},{96,112},{112,128},... | collective-permute-start | bytes 688136 | tf_op jit(solution)/shard_map/while/body/eval_jaxpr/ppermute | solution.py:17
  702.6 13.6 %collective-permute-start.1 = (bf16[32,3584]{1,0:T(8,128)(2,1)S(1)}, bf16[32,3584]{1,0:T(8,128)(2,1)S(1)}, u32[]{:S(2)}, u32[]{:S(2)}) collective-permute-start(bf16[32,3584]{1,0:T(8,128)(2,1)S(1)} %broadcast_select_fusion.5), channel_id=1, source_target_pairs={{0,16},{16,32},{32,48},{48,64},{64,80},{80,96},{96,112},{112,128},... | collective-permute-start | bytes 688136 | tf_op jit(solution)/shard_map/while/body/eval_jaxpr/ppermute | solution.py:17
  744.6 13.6 %all-to-all-start.1 = ((bf16[16,4,3584]{2,1,0:T(4,128)(2,1)}), bf16[16,4,3584]{2,1,0:T(4,128)(2,1)S(1)}, u32[]{:S(2)}, u32[]{:S(2)}) async-start(bf16[16,4,3584]{2,1,0:T(4,128)(2,1)} %reshape.179), calls=%async_computation.1 | async-start | bytes 917504 | tf_op jit(solution)/shard_map/while/body/eval_jaxpr/all_to_all | solution.py:75
  759.9 14.2 %collective-permute-start.1 = (bf16[32,3584]{1,0:T(8,128)(2,1)S(1)}, bf16[32,3584]{1,0:T(8,128)(2,1)S(1)}, u32[]{:S(2)}, u32[]{:S(2)}) collective-permute-start(bf16[32,3584]{1,0:T(8,128)(2,1)S(1)} %broadcast_select_fusion.5), channel_id=1, source_target_pairs={{0,16},{16,32},{32,48},{48,64},{64,80},{80,96},{96,112},{112,128},... | collective-permute-start | bytes 688136 | tf_op jit(solution)/shard_map/while/body/eval_jaxpr/ppermute | solution.py:17
  817.9 13.6 %collective-permute-start.1 = (bf16[32,3584]{1,0:T(8,128)(2,1)S(1)}, bf16[32,3584]{1,0:T(8,128)(2,1)S(1)}, u32[]{:S(2)}, u32[]{:S(2)}) collective-permute-start(bf16[32,3584]{1,0:T(8,128)(2,1)S(1)} %broadcast_select_fusion.5), channel_id=1, source_target_pairs={{0,16},{16,32},{32,48},{48,64},{64,80},{80,96},{96,112},{112,128},... | collective-permute-start | bytes 688136 | tf_op jit(solution)/shard_map/while/body/eval_jaxpr/ppermute | solution.py:17
  875.3 14.2 %collective-permute-start.1 = (bf16[32,3584]{1,0:T(8,128)(2,1)S(1)}, bf16[32,3584]{1,0:T(8,128)(2,1)S(1)}, u32[]{:S(2)}, u32[]{:S(2)}) collective-permute-start(bf16[32,3584]{1,0:T(8,128)(2,1)S(1)} %broadcast_select_fusion.5), channel_id=1, source_target_pairs={{0,16},{16,32},{32,48},{48,64},{64,80},{80,96},{96,112},{112,128},... | collective-permute-start | bytes 688136 | tf_op jit(solution)/shard_map/while/body/eval_jaxpr/ppermute | solution.py:17
  917.9 13.6 %all-to-all-start.1 = ((bf16[16,4,3584]{2,1,0:T(4,128)(2,1)}), bf16[16,4,3584]{2,1,0:T(4,128)(2,1)S(1)}, u32[]{:S(2)}, u32[]{:S(2)}) async-start(bf16[16,4,3584]{2,1,0:T(4,128)(2,1)} %reshape.179), calls=%async_computation.1 | async-start | bytes 917504 | tf_op jit(solution)/shard_map/while/body/eval_jaxpr/all_to_all | solution.py:75
  933.2 13.6 %collective-permute-start.1 = (bf16[32,3584]{1,0:T(8,128)(2,1)S(1)}, bf16[32,3584]{1,0:T(8,128)(2,1)S(1)}, u32[]{:S(2)}, u32[]{:S(2)}) collective-permute-start(bf16[32,3584]{1,0:T(8,128)(2,1)S(1)} %broadcast_select_fusion.5), channel_id=1, source_target_pairs={{0,16},{16,32},{32,48},{48,64},{64,80},{80,96},{96,112},{112,128},... | collective-permute-start | bytes 688136 | tf_op jit(solution)/shard_map/while/body/eval_jaxpr/ppermute | solution.py:17
  (28 other events, 315.2 us)
Sparse Core Ops, SparseCore 0:
  1000.3 82.4 reduce-scatter.3
where the time goes:
time: 1100 us; the launch traced here: 1090 us
  blocking collectives  301 us (27%)
  starting transfers between devices  253 us (23%)
  waiting for transfers between devices  243 us (22%)
  matrix products  159 us (14%)
  local copies, waits for them, and re-layouts  83.3 us (8%)
  other arithmetic  35.2 us (3%)
  between operations  13.4 us (1%)
    all_to_all x17, blocking collectives, advance(): lax.all_to_all(both, 'expert', split_axis=0, concat_axis=0, tiled=True)  301 us
    ppermute x34, starting transfers between devices, from_behind(): lax.ppermute(value, axis, [(source, source + steps) for source in range(i...  144 us
    all_to_all x17, waiting for transfers between devices, expert_rows(): lax.all_to_all(part, 'expert', split_axis=0, concat_axis=0, tiled=True)  122 us
    all_to_all x17, starting transfers between devices, expert_rows(): lax.all_to_all(part, 'expert', split_axis=0, concat_axis=0, tiled=True)  110 us
    unnamed x2, waiting for transfers between devices  82.6 us
    dot_general x17, matrix products, expert_rows(): jnp.dot(act, wdown, preferred_element_type=jnp.float32).astype(jnp.bfloat16)  78.4 us
    dot_general x17, matrix products, expert_rows(): gate = jnp.dot(rows, wgate, preferred_element_type=jnp.float32)  47.2 us
    ppermute x34, waiting for transfers between devices, from_behind(): lax.ppermute(value, axis, [(source, source + steps) for source in range(i...  38.7 us
  transfers between devices with their start and end apart: 52, of which 45 were waited for; matrix products, arithmetic and copies ran while one was open for 6% of the time, Pallas kernels for 0%

commit v1 on v0

v1 whole, which is shorter than its diff:
```python
import jax
import jax.numpy as jnp
from jax import lax
from jax.experimental import pallas as pl
from jax.experimental.pallas import tpu as pltpu
from jax.sharding import PartitionSpec as P

MESH = pl.DeviceIdType.MESH
BF16, F32 = jnp.bfloat16, jnp.float32

GROUP = 2
CAP = 2
FLOWS = 4
WIDE = 256

norm_eps = 1e-06
route_scale = 2.5


def home_of(flow, sec):
    y = lax.rem(sec // 4 + sec + flow, 4)
    return (flow // 2) * 8 + y * 2 + lax.rem(flow, 2)


def kernel(
    xin, gain, tab, wg_h, wu_h, wd_h, out,
    wg, wu, wd, ein, eout, part, act, hx, hrows, hparts, fin,
    rowtok, rowwt, coltok, chi, clo, place,
    w_sem, init_send, init_recv, ein_sem, eout_sem, rows_sem, parts_sem, fin_send, fin_recv,
):
    sections = lax.axis_size("section")
    spread = lax.axis_size("expert")
    window = spread // GROUP
    sec, exp = lax.axis_index("section"), lax.axis_index("expert")
    tokens = xin.shape[1]
    width = wg_h.shape[0]
    chunk = width // sections
    hid = wg_h.shape[1]
    last = sections - 1
    half = spread // 2

    weights = [
        pltpu.make_async_copy(src, dst, w_sem.at[k])
        for k, (src, dst) in enumerate(((wg_h, wg), (wu_h, wu), (wd_h, wd)))
    ]
    for copy in weights:
        copy.start()

    flow = jnp.int32(-1)
    for f in range(FLOWS):
        flow = jnp.where(home_of(f, sec) == exp, f, flow)
    is_home = flow >= 0
    flow = jnp.maximum(flow, 0)
    way, micro = flow // 2, lax.rem(flow, 2)

    for f in range(FLOWS):
        home = home_of(f, sec)

        @pl.when(home == exp)
        def _():
            pltpu.make_async_copy(xin.at[f], hx.at[exp], init_recv).start()

        @pl.when(home != exp)
        def _():
            pltpu.make_async_remote_copy(
                src_ref=xin.at[f], dst_ref=hx.at[exp], send_sem=init_send.at[f], recv_sem=init_recv,
                device_id=(sec, home), device_id_type=MESH,
            ).start()

    eout[...] = jnp.zeros_like(eout)

    slots = half * CAP * window
    lane = lax.broadcasted_iota(jnp.int32, (1, slots), 1)
    lane_block = lax.rem(lane // CAP, half)

    @pl.when(is_home)
    def _():
        source = lax.broadcasted_iota(jnp.int32, (tab.shape[1], slots), 0)
        column = (lane // (half * CAP)) * CAP + lax.rem(lane, CAP)
        rows = lax.broadcasted_iota(jnp.int32, (tab.shape[0], slots), 0)
        own = lax.rem(rows, half) == lane_block
        picked = []
        for kind in range(2):
            pick = (source == (flow * 2 + kind) * (window * CAP) + column).astype(F32)
            spread_out = jnp.dot(
                tab[...], pick, precision=lax.Precision.HIGHEST, preferred_element_type=F32
            )
            kept = jnp.where(own, spread_out, 0.0).reshape(sections * 2, half, slots)
            picked.append(jnp.sum(kept, axis=1))
        tok = picked[0]
        tok = jnp.where(tok < -0.5, -1.0, tok + (lane_block * tokens).astype(F32))
        rowtok[...] = tok
        rowwt[...] = picked[1]
        coltok[...] = tok.T

    def home_phase(i):
        layer = jnp.where(way == 0, i, last - i)
        before = jnp.where(way == 0, i - 1, last - i + 1)
        count = half * tokens
        for g in range(2):

            @pl.when(i > 0)
            def _():
                row = before * 2 + g
                wide = lax.broadcasted_iota(jnp.int32, (count, slots), 0).astype(F32)
                comb = jnp.where(wide == rowtok[pl.ds(row, 1), :], rowwt[pl.ds(row, 1), :], 0.0)
                high = comb.astype(BF16)
                low = (comb - high.astype(F32)).astype(BF16)
                chi[g] = jnp.concatenate([high, high], axis=1)
                clo[g] = jnp.concatenate([low, low], axis=1)

            @pl.when(i <= last)
            def _():
                col = coltok[...]
                at = lax.broadcasted_iota(jnp.int32, col.shape, 1) == layer * 2 + g
                own = jnp.sum(jnp.where(at, col, 0.0), axis=1, keepdims=True)
                wide = lax.broadcasted_iota(jnp.int32, (slots, count), 1).astype(F32)
                place[g] = (wide == own).astype(BF16)

        @pl.when(i == 0)
        def _():
            pltpu.make_async_copy(hx, hx, init_recv).wait()

        @pl.when(i > 0)
        def _():
            step = i - 1
            pltpu.make_async_copy(hparts.at[step], hparts.at[step], parts_sem.at[step]).wait()
            for g in range(2):
                got = hparts[step, :, g * half * CAP : (g + 1) * half * CAP, :]
                got = got.reshape(2 * slots, WIDE)
                added = jnp.dot(chi[g], got, preferred_element_type=F32)
                added += jnp.dot(clo[g], got, preferred_element_type=F32)
                old = hx[g * half : (g + 1) * half].reshape(count, WIDE)
                new = (old.astype(F32) + added).astype(BF16)
                hx[g * half : (g + 1) * half] = new.reshape(half, tokens, WIDE)

        @pl.when(i <= last)
        def _():
            for g in range(2):
                x = hx[g * half : (g + 1) * half].reshape(count, WIDE)
                rows = jnp.dot(place[g], x, preferred_element_type=F32).astype(BF16)
                hrows[i, :, g * half * CAP : (g + 1) * half * CAP, :] = rows.reshape(
                    window, half * CAP, WIDE
                )

            def send(e, unused):
                self_copy = (layer == sec) & (e == exp)

                @pl.when(self_copy)
                def _():
                    pltpu.make_async_copy(
                        hrows.at[i, e // GROUP], ein.at[flow, sec], ein_sem.at[flow, sec]
                    ).start()

                @pl.when(jnp.logical_not(self_copy))
                def _():
                    pltpu.make_async_remote_copy(
                        src_ref=hrows.at[i, e // GROUP], dst_ref=ein.at[flow, sec],
                        send_sem=rows_sem.at[i], recv_sem=ein_sem.at[flow, sec],
                        device_id=(layer, e), device_id_type=MESH,
                    ).start()

                return unused

            lax.fori_loop(0, spread, send, 0)

        @pl.when(i > last)
        def _():
            def send(b, unused):
                @pl.when(b == exp)
                def _():
                    pltpu.make_async_copy(hx.at[b], fin.at[flow], fin_recv.at[flow]).start()

                @pl.when(b != exp)
                def _():
                    pltpu.make_async_remote_copy(
                        src_ref=hx.at[b], dst_ref=fin.at[flow],
                        send_sem=fin_send, recv_sem=fin_recv.at[flow],
                        device_id=(sec, b), device_id_type=MESH,
                    ).start()

                return unused

            lax.fori_loop(0, spread, send, 0)

    def expert_phase(f, i):
        gate = jnp.zeros((spread * CAP, hid), F32)
        up = jnp.zeros((spread * CAP, hid), F32)
        square = jnp.zeros((spread * CAP, WIDE), F32)
        for c in range(sections):
            pltpu.make_async_copy(ein.at[f, c], ein.at[f, c], ein_sem.at[f, c]).wait()
            x = ein[f, c].astype(F32)
            square += x * x
            h = (x * gain[c : c + 1, :]).astype(BF16)[:, :chunk]
            rows = slice(c * chunk, (c + 1) * chunk)
            gate += jnp.dot(h, wg[rows, :], preferred_element_type=F32)
            up += jnp.dot(h, wu[rows, :], preferred_element_type=F32)
        scale = lax.rsqrt(jnp.sum(square, axis=1, keepdims=True) / width + norm_eps)
        gate = gate * scale
        up = up * scale
        act[...] = (gate / (1.0 + jnp.exp(-gate)) * up).astype(BF16)
        sent = 0
        mine = lax.rem(exp, GROUP) * window + exp // GROUP
        for lo in range(0, width, 256):
            hi = min(lo + 256, width)
            part[:, lo:hi] = jnp.dot(act[...], wd[:, lo:hi], preferred_element_type=F32).astype(BF16)
            while sent < sections and (sent + 1) * chunk <= hi:
                c = sent
                eout[f, c, :, :chunk] = part[:, c * chunk : (c + 1) * chunk]
                home = home_of(f, jnp.int32(c))
                self_copy = (c == sec) & (home == exp)

                @pl.when(self_copy)
                def _():
                    pltpu.make_async_copy(eout.at[f, c], hparts.at[i, mine], parts_sem.at[i]).start()

                @pl.when(jnp.logical_not(self_copy))
                def _():
                    pltpu.make_async_remote_copy(
                        src_ref=eout.at[f, c], dst_ref=hparts.at[i, mine],
                        send_sem=eout_sem.at[f], recv_sem=parts_sem.at[i],
                        device_id=(c, home), device_id_type=MESH,
                    ).start()

                sent += 1

    def step(t, unused):
        i = t - micro

        @pl.when(is_home & (i >= 0) & (i <= sections))
        def _():
            home_phase(i)

        @pl.when(t == jnp.minimum(sec, last - sec))
        def _():
            for copy in weights:
                copy.wait()

        def direction(d, unused):
            at = jnp.where(d == 0, sec, last - sec)
            m = t - at

            @pl.when((m >= 0) & (m < 2))
            def _():
                expert_phase(d * 2 + m, at)

            return unused

        lax.fori_loop(0, 2, direction, 0)
        return unused

    lax.fori_loop(0, sections + 2, step, 0)

    for f in range(FLOWS):
        pltpu.make_async_copy(fin.at[f], fin.at[f], fin_recv.at[f]).wait()
        out[f] = fin[f][:, :chunk]

    one = hx.at[0]
    for f in range(FLOWS):
        home = home_of(f, sec)

        @pl.when(home == exp)
        def _():
            pltpu.make_async_copy(eout.at[f, 1:], eout.at[f, 1:], eout_sem.at[f]).wait()

        @pl.when(home != exp)
        def _():
            pltpu.make_async_copy(eout.at[f], eout.at[f], eout_sem.at[f]).wait()
            pltpu.make_async_copy(one, one, init_send.at[f]).wait()

    @pl.when(is_home)
    def _():
        def drain(i, unused):
            layer = jnp.where(way == 0, i, last - i)

            @pl.when(layer == sec)
            def _():
                some = hparts.at[i, 1:]
                pltpu.make_async_copy(some, some, rows_sem.at[i]).wait()

            @pl.when(layer != sec)
            def _():
                pltpu.make_async_copy(hparts.at[i], hparts.at[i], rows_sem.at[i]).wait()

            return unused

        lax.fori_loop(0, sections, drain, 0)
        pltpu.make_async_copy(hx.at[1:], hx.at[1:], fin_send).wait()


def slot_table(ids, scores):
    flows, tokens, _ = ids.shape
    window = lax.axis_size("expert") // GROUP
    weights = route_scale * scores / jnp.sum(scores, axis=-1, keepdims=True)
    hit = (ids[:, :, :, None] == jnp.arange(window, dtype=jnp.int32)).astype(F32)
    count = jnp.sum(hit, axis=2)
    share = jnp.sum(weights[:, :, :, None] * hit, axis=2)
    earlier = (jnp.arange(tokens)[:, None] > jnp.arange(tokens)[None, :]).astype(F32)
    before = jnp.sum(earlier[None, :, :, None] * count[:, None, :, :], axis=2)
    slot = jnp.arange(CAP, dtype=F32)
    place = count[..., None] * (before[..., None] == slot).astype(F32)
    number = jnp.arange(1, tokens + 1, dtype=F32)
    tok = jnp.sum(place * number[None, :, None, None], axis=1) - 1.0
    weight = jnp.sum(place * share[..., None], axis=1)
    return jnp.stack([tok, weight], axis=1).reshape(1, -1)


def on_device(entering, norm_gain, w_gate, w_up, w_down, route_ids, route_scores):
    sections = lax.axis_size("section")
    spread = lax.axis_size("expert")
    sec = lax.axis_index("section")
    tokens, width = entering.shape[2:]
    chunk = width // sections
    hid = w_gate.shape[2]
    pad = WIDE - chunk
    xin = lax.dynamic_slice_in_dim(entering, sec * chunk, chunk, 3).reshape(FLOWS, tokens, chunk)
    xin = jnp.pad(xin, ((0, 0), (0, 0), (0, pad)))
    gain = jnp.pad(norm_gain.reshape(sections, chunk), ((0, 0), (0, pad)))
    own = slot_table(
        route_ids[:, :, 0].reshape(FLOWS, tokens, -1), route_scores[:, :, 0].reshape(FLOWS, tokens, -1)
    )
    tab = lax.all_gather(own, ("section", "expert"), axis=0, tiled=True)
    slots = spread * CAP * spread // GROUP // 2
    count = spread // 2 * tokens
    vmem = pl.BlockSpec(memory_space=pltpu.VMEM)
    hbm = pl.BlockSpec(memory_space=pl.ANY)
    out = pl.pallas_call(
        kernel,
        out_shape=jax.ShapeDtypeStruct((FLOWS, tokens, chunk), BF16),
        in_specs=[vmem, vmem, vmem, hbm, hbm, hbm],
        out_specs=vmem,
        scratch_shapes=[
            pltpu.VMEM((width, hid), BF16),
            pltpu.VMEM((width, hid), BF16),
            pltpu.VMEM((hid, width), BF16),
            pltpu.VMEM((FLOWS, sections, spread * CAP, WIDE), BF16),
            pltpu.VMEM((FLOWS, sections, spread * CAP, WIDE), BF16),
            pltpu.VMEM((spread * CAP, width), BF16),
            pltpu.VMEM((spread * CAP, hid), BF16),
            pltpu.VMEM((spread, tokens, WIDE), BF16),
            pltpu.VMEM((sections, spread // GROUP, spread * CAP, WIDE), BF16),
            pltpu.VMEM((sections, spread, spread * CAP, WIDE), BF16),
            pltpu.VMEM((FLOWS, tokens, WIDE), BF16),
            pltpu.VMEM((sections * 2, slots), F32),
            pltpu.VMEM((sections * 2, slots), F32),
            pltpu.VMEM((slots, sections * 2), F32),
            pltpu.VMEM((2, count, 2 * slots), BF16),
            pltpu.VMEM((2, count, 2 * slots), BF16),
            pltpu.VMEM((2, slots, count), BF16),
            pltpu.SemaphoreType.DMA((3,)),
            pltpu.SemaphoreType.DMA((FLOWS,)),
            pltpu.SemaphoreType.DMA,
            pltpu.SemaphoreType.DMA((FLOWS, sections)),
            pltpu.SemaphoreType.DMA((FLOWS,)),
            pltpu.SemaphoreType.DMA((sections,)),
            pltpu.SemaphoreType.DMA((sections,)),
            pltpu.SemaphoreType.DMA,
            pltpu.SemaphoreType.DMA((FLOWS,)),
        ],
        compiler_params=pltpu.CompilerParams(
            has_side_effects=True, vmem_limit_bytes=48 * 2**20
        ),
        cost_estimate=pl.CostEstimate(
            flops=2 * FLOWS * spread * CAP * width * hid * 3,
            bytes_accessed=width * hid * 6,
            transcendentals=0,
        ),
        name="relay",
    )(xin, gain, tab, w_gate[0], w_up[0], w_down[0])
    return out.reshape(2, 2, tokens, chunk)


def solution(mesh):
    return jax.shard_map(
        on_device,
        mesh=mesh,
        in_specs=(
            P(None, None, "expert", None),
            P("section", None),
            P("section", None, "expert"),
            P("section", None, "expert"),
            P("section", "expert", None),
            P(None, None, "section", "expert", None),
            P(None, None, "section", "expert", None),
        ),
        out_specs=P(None, None, "expert", "section"),
        check_vma=False,
    )
```

time: 1100 us -> 450 us (0.41)
  Pallas kernels: 0 us -> 384 us
  starting transfers between devices: 253 us -> 0 us
  blocking collectives: 301 us -> 56.9 us
  waiting for transfers between devices: 243 us -> 0 us
  matrix products: 159 us -> 0 us
  local copies, waits for them, and re-layouts: 83.3 us -> 3.2 us
  other arithmetic: 35.2 us -> 2.68 us
  between operations: 13.4 us -> 0.08 us
    pallas_call x0 -> x1, Pallas kernels: none -> 384 us  [on_device(): pl.pallas_call(kernel, out_shape=jax.ShapeDtypeStruct((FLOWS, tokens, chu...]
    all_to_all x17 -> x0, blocking collectives: 301 us -> none  [advance(): lax.all_to_all(both, 'expert', split_axis=0, concat_axis=0, tiled=True)]
    dot_general x136 -> x0, matrix products: 159 us -> none  [the longest x17 78.4 us: expert_rows(): jnp.dot(act, wdown, preferred_element_type=jnp.float32).astype(jnp.bfloat16)]
    ppermute x34 -> x0, starting transfers between devices: 144 us -> none  [from_behind(): lax.ppermute(value, axis, [(source, source + steps) for source in range(i...]
    all_to_all x17 -> x0, waiting for transfers between devices: 122 us -> none  [expert_rows(): lax.all_to_all(part, 'expert', split_axis=0, concat_axis=0, tiled=True)]
    all_to_all x17 -> x0, starting transfers between devices: 110 us -> none  [expert_rows(): lax.all_to_all(part, 'expert', split_axis=0, concat_axis=0, tiled=True)]
    unnamed x2 -> x0, waiting for transfers between devices: 82.6 us -> none
    all_gather x0 -> x1, blocking collectives: none -> 56.9 us  [on_device(): tab = lax.all_gather(own, ('section', 'expert'), axis=0, tiled=True)]
  transfers between devices with their start and end apart: 52 -> 0, of which waited for: 45 -> 0; matrix products, arithmetic and copies ran while one was open for 6% -> 0% of each run, Pallas kernels for 0% -> 0%
where the time goes in v1:
time: 450 us; the launch traced here: 447 us
  Pallas kernels  384 us (85%)
  blocking collectives  56.9 us (13%)
    pallas_call x1, Pallas kernels, on_device(): pl.pallas_call(kernel, out_shape=jax.ShapeDtypeStruct((FLOWS, tokens, chu...  384 us
    all_gather x1, blocking collectives, on_device(): tab = lax.all_gather(own, ('section', 'expert'), axis=0, tiled=True)  56.9 us

profile of v1, /device:TPU:61, one launch (start us, length us, event | category | flops | bytes accessed | tf_op | source)
XLA Modules:
  0.0 446.9 jit_solution(818237145678720761)
XLA Ops:
  0.0 0.0 copy-start
  0.0 0.8 reduce.1
  0.8 0.1 reshape.56
  0.9 0.7 fusion.4
  1.7 0.8 convert_reduce_fusion
  2.5 0.2 multiply_reduce_fusion
  2.7 0.1 copy.23
  2.7 0.1 fusion
  2.9 0.1 copy.26
  3.0 0.1 reshape.59
  3.1 0.0 copy-done
  3.2 0.1 constant_dynamic-slice_fusion
  3.3 56.9 %all-gather = f32[256,1,128]{2,1,0:T(1,128)S(1)} all-gather(f32[1,1,128]{2,1,0:T(1,128)S(1)} %reshape.59), channel_id=1, replica_groups=mesh['section'=16,'expert'=16] {'section','expert'}, dimensions={0}, use_global_device_ids=true | all-gather | bytes 131584 | tf_op jit(solution)/shard_map/all_gather | solution.py:322
  60.2 0.0 copy-start.1
  60.2 2.0 copy-done.1
  62.2 384.1 %relay.1 = bf16[4,32,224]{2,1,0:T(8,128)(2,1)S(1)} custom-call(bf16[4,32,256]{2,1,0:T(8,128)(2,1)S(1)} %pad.8.xin, f32[16,256]{1,0:T(8,128)S(1)} %pad.9.gain, f32[256,128]{1,0:T(8,128)S(1)} %bitcast.17, bf16[3584,512]{1,0:T(8,128)(2,1)S(1)} %bitcast.16, bf16[3584,512]{1,0:T(8,128)(2,1)} %bitcast.19, bf16[512,3584]{1,0:T(8,128)(2,1)} %bitcast.20), custom_call_target="tpu_custom_call" | custom-call | flops 1409286144 | bytes 11010048 | tf_op jit(solution)/shard_map/relay/pallas_call | solution.py:327
  446.3 0.6 copy.32
  (7 shorter events, 0.1 us)
Async XLA Ops:
  0.0 3.1 copy-start
  60.2 2.0 copy-start.1

commit v2 on v0

v2 whole, which is shorter than its diff:
```python
import jax
import jax.numpy as jnp
from jax import lax
from jax.experimental import pallas as pl
from jax.experimental.pallas import tpu as pltpu
from jax.sharding import PartitionSpec as P

MESH = pl.DeviceIdType.MESH
BF16, F32 = jnp.bfloat16, jnp.float32

GROUP = 2
CAP = 2
FLOWS = 4
WIDE = 256
NZ = 4
NY = 4

norm_eps = 1e-06
route_scale = 2.5


def home_of(flow, x, y):
    return lax.rem(x + y + flow // 2, 2) * (2 * NY) + y * 2 + flow % 2


def iota(shape, dim):
    return lax.broadcasted_iota(jnp.int32, shape, dim)


def kernel(
    entering, norm_gain, wg_h, wu_h, wd_h, ids, scores, out,
    wg, wu, wd, raw, xin, gain, ein, eout, part, act,
    hx, hnew, hrows, hparts, fin, tabrow, tab, chi, clo, place,
    w_sem, raw_sem, init_send, init_recv, ein_sem, eout_sem, rows_sem, parts_sem,
    move_send, move_recv, fin_send, fin_recv, tab_send, tab_recv,
):
    sections = lax.axis_size("section")
    spread = lax.axis_size("expert")
    window = spread // GROUP
    nx = sections // NZ
    sec, exp = lax.axis_index("section"), lax.axis_index("expert")
    my_x, my_z = sec // NZ, lax.rem(sec, NZ)
    my_y = lax.rem(exp // 2, NY)
    tokens = ids.shape[3]
    width = wg_h.shape[1]
    chunk = width // sections
    block = chunk * NY
    hid = wg_h.shape[2]
    last = sections - 1
    half = spread // 2
    slots = half * CAP * window
    count = half * tokens

    flow = lax.rem(exp // (2 * NY) + my_x + my_y, 2) * 2 + lax.rem(exp, 2)
    way = flow // 2
    my_chunk = my_x * NY + my_y
    starts = my_z == way * (NZ - 1)
    ends = my_z == (1 - way) * (NZ - 1)
    first_visit = way * (nx - 1)

    def send(src, dst, send_sem, recv_sem, section, device):
        here = (section == sec) & (device == exp)

        @pl.when(here)
        def _():
            pltpu.make_async_copy(src, dst, recv_sem).start()

        @pl.when(jnp.logical_not(here))
        def _():
            pltpu.make_async_remote_copy(
                src_ref=src, dst_ref=dst, send_sem=send_sem, recv_sem=recv_sem,
                device_id=(section, device), device_id_type=MESH,
            ).start()

    def sent(src, send_sem, section, device):
        @pl.when(jnp.logical_not((section == sec) & (device == exp)))
        def _():
            pltpu.make_async_copy(src, src, send_sem).wait()

    def arrived(ref, sem):
        pltpu.make_async_copy(ref, ref, sem).wait()

    mine_in = entering.at[:, :, :, pl.ds(pl.multiple_of(my_x * block, 128), block)]
    fetch = pltpu.make_async_copy(mine_in, raw, raw_sem)
    fetch.start()
    weights = [
        pltpu.make_async_copy(src.at[0], dst, w_sem.at[k])
        for k, (src, dst) in enumerate(((wg_h, wg), (wu_h, wu), (wd_h, wd)))
    ]

    lanes = FLOWS * 2 * window * CAP
    lane = iota((1, lanes), 1)
    lane_expert = lax.rem(lane // CAP, window)
    lane_slot = lax.rem(lane, CAP).astype(F32)
    lane_kind = lax.rem(lane // (CAP * window), 2)
    lane_flow = lane // (2 * CAP * window)
    earlier = (iota((tokens, tokens), 0) > iota((tokens, tokens), 1)).astype(BF16)
    number = iota((tokens, lanes), 0).astype(F32) + 1.0
    table = jnp.zeros((1, lanes), F32)
    for f in range(FLOWS):
        chosen = ids[f // 2, f % 2, 0]
        score = scores[f // 2, f % 2, 0]
        weight = route_scale * score / jnp.sum(score, axis=1, keepdims=True)
        hit = jnp.zeros((tokens, lanes), F32)
        share = jnp.zeros((tokens, lanes), F32)
        for k in range(chosen.shape[1]):
            same = chosen[:, k : k + 1] == lane_expert
            hit += jnp.where(same, 1.0, 0.0)
            share += jnp.where(same, weight[:, k : k + 1], 0.0)
        before = jnp.dot(earlier, hit.astype(BF16), preferred_element_type=F32)
        held = jnp.where(before == lane_slot, hit, 0.0)
        value = jnp.where(lane_kind == 0, number, share)
        row = jnp.sum(held * value, axis=0, keepdims=True) - jnp.where(lane_kind == 0, 1.0, 0.0)
        table += jnp.where(lane_flow == f, row, 0.0)
    tabrow[0] = table

    def tables(deliver):
        for f in range(FLOWS):
            d = f // 2
            prior = sec + (2 * d - 1)

            def one(c, unused):
                x, y = c // NY, lax.rem(c, NY)
                device = home_of(f, x, y)

                @pl.when(sec == d * last)
                def _():
                    deliver(2 * nx, x * NZ + my_z, device)

                @pl.when((prior >= 0) & (prior <= last))
                def _():
                    deliver(nx + prior // NZ, x * NZ + lax.rem(prior, NZ), device)

                deliver(my_x, x * NZ + my_z, device)
                return unused

            lax.fori_loop(0, sections, one, 0)

    def deliver_table(use, section, device):
        send(tabrow.at[0], tab.at[use, exp], tab_send, tab_recv.at[use], section, device)

    def drain_table(use, section, device):
        sent(tabrow.at[0], tab_send, section, device)

    fetch.wait()

    def enter(act_on):
        for f in range(FLOWS):
            d, m = f // 2, f % 2

            @pl.when(my_z == d * (NZ - 1))
            def _():
                for y in range(NY):
                    act_on(f, d, m, y, home_of(f, my_x, y))

    def send_entering(f, d, m, y, device):
        xin[m, y] = jnp.zeros((tokens, WIDE), BF16)
        xin[m, y, :, :chunk] = raw[d, m, :, y * chunk : (y + 1) * chunk]
        send(xin.at[m, y], hx.at[d * (nx - 1), exp], init_send.at[m, y], init_recv, sec, device)

    def sent_entering(f, d, m, y, device):
        sent(xin.at[m, y], init_send.at[m, y], sec, device)

    enter(send_entering)
    tables(deliver_table)
    for copy in weights:
        copy.start()
    eout[...] = jnp.zeros_like(eout)
    for c in range(sections):
        gain[c : c + 1, :] = jnp.zeros((1, WIDE), F32)
        gain[c : c + 1, :chunk] = norm_gain[:, c * chunk : (c + 1) * chunk]

    spot = iota((1, slots), 1)
    spot_lane = (spot // (half * CAP)) * CAP + lax.rem(spot, CAP)
    spot_block = lax.rem(spot // CAP, half)

    def pick(kind):
        return (iota((lanes, slots), 0) == (flow * 2 + kind) * (window * CAP) + spot_lane).astype(F32)

    def rows_of(use, kind):
        got = jnp.concatenate([tab[use, b] for b in range(spread)], axis=0)
        wide = jnp.dot(got, pick(kind), precision=lax.Precision.HIGHEST, preferred_element_type=F32)
        own = lax.rem(iota((spread, slots), 0), half) == spot_block
        kept = jnp.where(own, wide, 0.0)
        return [jnp.sum(kept[g * half : (g + 1) * half], axis=0, keepdims=True) for g in range(2)]

    def prepare_sums(use):
        arrived(tab.at[use], tab_recv.at[use])
        toks, shares = rows_of(use, 0), rows_of(use, 1)
        for g in range(2):
            tok = jnp.where(toks[g] < -0.5, -1.0, toks[g] + (spot_block * tokens).astype(F32))
            comb = jnp.where(iota((count, slots), 0).astype(F32) == tok, shares[g], 0.0)
            high = comb.astype(BF16)
            low = (comb - high.astype(F32)).astype(BF16)
            chi[g] = jnp.concatenate([high, high], axis=1)
            clo[g] = jnp.concatenate([low, low], axis=1)

    def prepare_rows(use):
        arrived(tab.at[use], tab_recv.at[use])
        toks = rows_of(use, 0)
        for g in range(2):
            tok = jnp.where(toks[g] < -0.5, -1.0, toks[g] + (spot_block * tokens).astype(F32))
            col = jnp.broadcast_to(tok, (slots, slots)).T[:, :1]
            place[g] = (iota((slots, count), 1).astype(F32) == col).astype(BF16)

    def dispatch(source, k, layer):
        for g in range(2):
            x = source[g * half : (g + 1) * half].reshape(count, WIDE)
            rows = jnp.dot(place[g], x, preferred_element_type=F32).astype(BF16)
            hrows[k, :, g * half * CAP : (g + 1) * half * CAP, :] = rows.reshape(
                window, half * CAP, WIDE
            )

        def one(e, unused):
            send(
                hrows.at[k, e // GROUP], ein.at[flow, my_chunk],
                rows_sem.at[k], ein_sem.at[flow, my_chunk], layer, e,
            )
            return unused

        lax.fori_loop(0, spread, one, 0)

    @pl.when(starts)
    def _():
        prepare_rows(2 * nx)
        arrived(hx.at[first_visit], init_recv)
        dispatch(hx[first_visit], nx, way * last)

    tables(drain_table)
    enter(sent_entering)

    around = sorted(
        ((dx, dy) for dx in range(nx) for dy in range(NY)),
        key=lambda o: (min(o[0], nx - o[0]) + min(o[1], NY - o[1]), o),
    )
    columns = sorted(range(nx), key=lambda dx: -min(dx, nx - dx))

    def expert_phase(f):
        gate = jnp.zeros((spread * CAP, hid), F32)
        up = jnp.zeros((spread * CAP, hid), F32)
        square = jnp.zeros((spread * CAP, WIDE), F32)
        for dx, dy in around:
            c = lax.rem(my_x + dx, nx) * NY + lax.rem(my_y + dy, NY)
            arrived(ein.at[f, c], ein_sem.at[f, c])
            x = ein[f, c].astype(F32)
            square += x * x
            h = (x * gain[pl.ds(c, 1), :]).astype(BF16)[:, :chunk]
            rows = pl.ds(pl.multiple_of(c * chunk, 32), chunk)
            gate += jnp.dot(h, wg[rows, :], preferred_element_type=F32)
            up += jnp.dot(h, wu[rows, :], preferred_element_type=F32)
        scale = lax.rsqrt(jnp.sum(square, axis=1, keepdims=True) / width + norm_eps)
        gate = gate * scale
        up = up * scale
        act[...] = (gate / (1.0 + jnp.exp(-gate)) * up).astype(BF16)
        mine = lax.rem(exp, GROUP) * window + exp // GROUP
        for dx in columns:
            x = lax.rem(my_x + dx, nx)
            cols = pl.ds(pl.multiple_of(x * block, 128), block)
            part[...] = jnp.dot(act[...], wd[:, cols], preferred_element_type=F32).astype(BF16)
            for y in range(NY):
                c = x * NY + y
                eout[f, c, :, :chunk] = part[:, y * chunk : (y + 1) * chunk]
                send(
                    eout.at[f, c], hparts.at[my_x, mine], eout_sem.at[f], parts_sem.at[my_x],
                    x * NZ + my_z, home_of(f, x, y),
                )

    def home_phase(k, layer):
        following = layer + 1 - 2 * way
        onward = (following >= 0) & (following <= last)
        prepare_sums(k)

        @pl.when(onward)
        def _():
            prepare_rows(nx + k)

        @pl.when(jnp.logical_not(starts & (k == first_visit)))
        def _():
            arrived(hx.at[k], move_recv.at[k])

        arrived(hparts.at[k], parts_sem.at[k])
        for g in range(2):
            got = hparts[k, :, g * half * CAP : (g + 1) * half * CAP, :]
            got = got.reshape(2 * slots, WIDE)
            added = jnp.dot(chi[g], got, preferred_element_type=F32)
            added += jnp.dot(clo[g], got, preferred_element_type=F32)
            old = hx[k, g * half : (g + 1) * half].reshape(count, WIDE)
            new = (old.astype(F32) + added).astype(BF16)
            hnew[k, g * half : (g + 1) * half] = new.reshape(half, tokens, WIDE)

        @pl.when(onward)
        def _():
            dispatch(hnew[k], k, following)
            pltpu.make_async_remote_copy(
                src_ref=hnew.at[k], dst_ref=hx.at[following // NZ],
                send_sem=move_send.at[k], recv_sem=move_recv.at[following // NZ],
                device_id=(my_x * NZ + lax.rem(following, NZ), exp), device_id_type=MESH,
            ).start()

        @pl.when(jnp.logical_not(onward))
        def _():
            def one(b, unused):
                send(hnew.at[k, b], fin.at[flow], fin_send, fin_recv.at[flow], my_chunk, b)
                return unused

            lax.fori_loop(0, spread, one, 0)

    def step(t, unused):
        @pl.when(t == jnp.minimum(sec, last - sec))
        def _():
            for copy in weights:
                copy.wait()

        def direction(d, unused):
            @pl.when(t == jnp.where(d == 0, sec, last - sec))
            def _():
                def micro(m, unused):
                    expert_phase(d * 2 + m)
                    return unused

                lax.fori_loop(0, 2, micro, 0)

            return unused

        lax.fori_loop(0, 2, direction, 0)
        layer = jnp.where(way == 0, t, last - t)

        @pl.when(lax.rem(layer, NZ) == my_z)
        def _():
            home_phase(layer // NZ, layer)

        return unused

    lax.fori_loop(0, sections, step, 0)

    for f in range(FLOWS):

        @pl.when(f == flow)
        def _():
            arrived(eout.at[f, 1:], eout_sem.at[f])

        @pl.when(f != flow)
        def _():
            arrived(eout.at[f], eout_sem.at[f])

    for k in range(nx):
        final = ends & (k == (1 - way) * (nx - 1))

        @pl.when(jnp.logical_not(final))
        def _():
            arrived(hparts.at[k], rows_sem.at[k])
            arrived(hnew.at[k], move_send.at[k])

        @pl.when(final)
        def _():
            lax.fori_loop(
                0, spread, lambda b, unused: (sent(hnew.at[k, 0], fin_send, my_chunk, b), unused)[1], 0
            )

    @pl.when(starts)
    def _():
        lax.fori_loop(
            0, spread, lambda e, unused: (sent(hrows.at[nx, 0], rows_sem.at[nx], way * last, e), unused)[1], 0
        )

    for f in range(FLOWS):
        arrived(fin.at[f], fin_recv.at[f])
        out[f // 2, f % 2] = fin[f][:, :chunk]


def on_device(entering, norm_gain, w_gate, w_up, w_down, route_ids, route_scores):
    sections = lax.axis_size("section")
    spread = lax.axis_size("expert")
    tokens, width = entering.shape[2:]
    chunk = width // sections
    hid = w_gate.shape[2]
    nx = sections // NZ
    window = spread // GROUP
    rows = spread * CAP
    slots = spread // 2 * CAP * window
    count = spread // 2 * tokens
    lanes = FLOWS * 2 * window * CAP
    vmem = pl.BlockSpec(memory_space=pltpu.VMEM)
    hbm = pl.BlockSpec(memory_space=pl.ANY)
    dma = pltpu.SemaphoreType.DMA
    return pl.pallas_call(
        kernel,
        out_shape=jax.ShapeDtypeStruct((2, 2, tokens, chunk), BF16),
        in_specs=[hbm, vmem, hbm, hbm, hbm, vmem, vmem],
        out_specs=vmem,
        scratch_shapes=[
            pltpu.VMEM((width, hid), BF16),
            pltpu.VMEM((width, hid), BF16),
            pltpu.VMEM((hid, width), BF16),
            pltpu.VMEM((2, 2, tokens, chunk * NY), BF16),
            pltpu.VMEM((2, NY, tokens, WIDE), BF16),
            pltpu.VMEM((sections, WIDE), F32),
            pltpu.VMEM((FLOWS, sections, rows, WIDE), BF16),
            pltpu.VMEM((FLOWS, sections, rows, WIDE), BF16),
            pltpu.VMEM((rows, chunk * NY), BF16),
            pltpu.VMEM((rows, hid), BF16),
            pltpu.VMEM((nx, spread, tokens, WIDE), BF16),
            pltpu.VMEM((nx, spread, tokens, WIDE), BF16),
            pltpu.VMEM((nx + 1, window, rows, WIDE), BF16),
            pltpu.VMEM((nx, spread, rows, WIDE), BF16),
            pltpu.VMEM((FLOWS, tokens, WIDE), BF16),
            pltpu.VMEM((1, 1, lanes), F32),
            pltpu.VMEM((2 * nx + 1, spread, 1, lanes), F32),
            pltpu.VMEM((2, count, 2 * slots), BF16),
            pltpu.VMEM((2, count, 2 * slots), BF16),
            pltpu.VMEM((2, slots, count), BF16),
            dma((3,)),
            dma,
            dma((2, NY)),
            dma,
            dma((FLOWS, sections)),
            dma((FLOWS,)),
            dma((nx + 1,)),
            dma((nx,)),
            dma((nx,)),
            dma((nx,)),
            dma,
            dma((FLOWS,)),
            dma,
            dma((2 * nx + 1,)),
        ],
        compiler_params=pltpu.CompilerParams(
            has_side_effects=True, vmem_limit_bytes=48 * 2**20
        ),
        cost_estimate=pl.CostEstimate(
            flops=2 * FLOWS * rows * width * hid * 3,
            bytes_accessed=width * hid * 6,
            transcendentals=0,
        ),
        name="relay",
    )(entering, norm_gain, w_gate, w_up, w_down, route_ids, route_scores)


def solution(mesh):
    return jax.shard_map(
        on_device,
        mesh=mesh,
        in_specs=(
            P(None, None, "expert", None),
            P("section", None),
            P("section", None, "expert"),
            P("section", None, "expert"),
            P("section", "expert", None),
            P(None, None, "section", "expert", None),
            P(None, None, "section", "expert", None),
        ),
        out_specs=P(None, None, "expert", "section"),
        check_vma=False,
    )
```

time: 1100 us -> 340 us (0.31)
  Pallas kernels: 0 us -> 330 us
  blocking collectives: 301 us -> 0 us
  starting transfers between devices: 253 us -> 0 us
  waiting for transfers between devices: 243 us -> 0 us
  matrix products: 159 us -> 0 us
  local copies, waits for them, and re-layouts: 83.3 us -> 6.15 us
  other arithmetic: 35.2 us -> 0 us
  between operations: 13.4 us -> 0.02 us
    pallas_call x0 -> x1, Pallas kernels: none -> 330 us  [on_device(): pl.pallas_call(kernel, out_shape=jax.ShapeDtypeStruct((2, 2, tokens, chun...]
    all_to_all x17 -> x0, blocking collectives: 301 us -> none  [advance(): lax.all_to_all(both, 'expert', split_axis=0, concat_axis=0, tiled=True)]
    dot_general x136 -> x0, matrix products: 159 us -> none  [the longest x17 78.4 us: expert_rows(): jnp.dot(act, wdown, preferred_element_type=jnp.float32).astype(jnp.bfloat16)]
    ppermute x34 -> x0, starting transfers between devices: 144 us -> none  [from_behind(): lax.ppermute(value, axis, [(source, source + steps) for source in range(i...]
    all_to_all x17 -> x0, waiting for transfers between devices: 122 us -> none  [expert_rows(): lax.all_to_all(part, 'expert', split_axis=0, concat_axis=0, tiled=True)]
    all_to_all x17 -> x0, starting transfers between devices: 110 us -> none  [expert_rows(): lax.all_to_all(part, 'expert', split_axis=0, concat_axis=0, tiled=True)]
    unnamed x2 -> x0, waiting for transfers between devices: 82.6 us -> none
    slice x68 -> x0, local copies, waits for them, and re-layouts: 48.4 us -> none  [the longest x17 21 us: advance(): entering[1]]
  transfers between devices with their start and end apart: 52 -> 0, of which waited for: 45 -> 0; matrix products, arithmetic and copies ran while one was open for 6% -> 0% of each run, Pallas kernels for 0% -> 0%
where the time goes in v2:
time: 340 us; the launch traced here: 336 us
  Pallas kernels  330 us (97%)
  local copies, waits for them, and re-layouts  6.15 us (2%)
    pallas_call x1, Pallas kernels, on_device(): pl.pallas_call(kernel, out_shape=jax.ShapeDtypeStruct((2, 2, tokens, chun...  330 us

profile of v2, /device:TPU:61, one launch (start us, length us, event | category | flops | bytes accessed | tf_op | source)
XLA Modules:
  0.0 335.8 jit_solution(8433423593419289670)
XLA Ops:
  0.0 0.8 copy.8.ids
  0.8 0.8 copy.9.scores
  1.6 0.0 copy-start
  1.6 2.0 copy-done
  3.6 0.0 copy-start.1
  3.6 1.2 copy-done.1
  4.8 0.0 copy-start.2
  4.8 0.7 copy-done.2
  5.5 329.6 %relay.1 = bf16[2,2,32,224]{3,2,1,0:T(8,128)(2,1)S(1)} custom-call(bf16[2,2,32,3584]{3,2,1,0:T(8,128)(2,1)S(1)} %copy-done.1, f32[1,3584]{1,0:T(1,128)S(1)} %copy-done.2, bf16[1,3584,512]{2,1,0:T(8,128)(2,1)S(1)} %copy-done, bf16[1,3584,512]{2,1,0:T(8,128)(2,1)} %wu_h.1, bf16[1,512,3584]{2,1,0:T(8,128)(2,1)} %wd_h.1, s32[2,2,1,32,8]{4,3,2,1,0:T(8,128)S(1)} %copy.8.ids, ...), custom_call_target="tpu_custom_call" | custom-call | flops 1409286144 | bytes 11010048 | tf_op jit(solution)/shard_map/relay/pallas_call | solution.py:386
  335.2 0.6 copy.11
Async XLA Ops:
  1.6 2.0 copy-start
  3.6 1.2 copy-start.1
  4.8 0.7 copy-start.2

commit v3 on v2

--- a/solution.py
+++ b/solution.py
@@ -14,6 +14,7 @@
 WIDE = 256
 NZ = 4
 NY = 4
+FAR = 9
 
 norm_eps = 1e-06
 route_scale = 2.5
@@ -28,9 +29,10 @@
 
 
 def kernel(
-    entering, norm_gain, wg_h, wu_h, wd_h, ids, scores, out,
+    entering, gain_h, wg_h, wu_h, wd_h, ids_h, scores_h, out,
     wg, wu, wd, raw, xin, gain, ein, eout, part, act,
     hx, hnew, hrows, hparts, fin, tabrow, tab, chi, clo, place,
+    turn, norm_gain, ids, scores, gain_sem, eswap, pin, swap_send, pin_sem, pass_send,
     w_sem, raw_sem, init_send, init_recv, ein_sem, eout_sem, rows_sem, parts_sem,
     move_send, move_recv, fin_send, fin_recv, tab_send, tab_recv,
 ):
@@ -41,7 +43,7 @@
     sec, exp = lax.axis_index("section"), lax.axis_index("expert")
     my_x, my_z = sec // NZ, lax.rem(sec, NZ)
     my_y = lax.rem(exp // 2, NY)
-    tokens = ids.shape[3]
+    tokens = ids.shape[4]
     width = wg_h.shape[1]
     chunk = width // sections
     block = chunk * NY
@@ -82,11 +84,22 @@
 
     mine_in = entering.at[:, :, :, pl.ds(pl.multiple_of(my_x * block, 128), block)]
     fetch = pltpu.make_async_copy(mine_in, raw, raw_sem)
+    small = [
+        pltpu.make_async_copy(src, dst, gain_sem.at[k])
+        for k, (src, dst) in enumerate(((ids_h, ids), (scores_h, scores), (gain_h, norm_gain)))
+    ]
+    for copy in small:
+        copy.start()
     fetch.start()
     weights = [
         pltpu.make_async_copy(src.at[0], dst, w_sem.at[k])
         for k, (src, dst) in enumerate(((wg_h, wg), (wu_h, wu), (wd_h, wd)))
     ]
+
+    for copy in weights:
+        copy.start()
+    for copy in small:
+        copy.wait()
 
     lanes = FLOWS * 2 * window * CAP
     lane = iota((1, lanes), 1)
@@ -98,8 +111,8 @@
     number = iota((tokens, lanes), 0).astype(F32) + 1.0
     table = jnp.zeros((1, lanes), F32)
     for f in range(FLOWS):
-        chosen = ids[f // 2, f % 2, 0]
-        score = scores[f // 2, f % 2, 0]
+        chosen = ids[f // 2, f % 2, 0].T
+        score = scores[f // 2, f % 2, 0].T
         weight = route_scale * score / jnp.sum(score, axis=1, keepdims=True)
         hit = jnp.zeros((tokens, lanes), F32)
         share = jnp.zeros((tokens, lanes), F32)
@@ -114,7 +127,7 @@
         table += jnp.where(lane_flow == f, row, 0.0)
     tabrow[0] = table
 
-    def tables(deliver):
+    def tables(deliver, first):
         for f in range(FLOWS):
             d = f // 2
             prior = sec + (2 * d - 1)
@@ -123,9 +136,9 @@
                 x, y = c // NY, lax.rem(c, NY)
                 device = home_of(f, x, y)
 
-                @pl.when(sec == d * last)
-                def _():
+                if first:
                     deliver(2 * nx, x * NZ + my_z, device)
+                    return unused
 
                 @pl.when((prior >= 0) & (prior <= last))
                 def _():
@@ -134,7 +147,14 @@
                 deliver(my_x, x * NZ + my_z, device)
                 return unused
 
-            lax.fori_loop(0, sections, one, 0)
+            if first:
+
+                @pl.when(sec == d * last)
+                def _():
+                    lax.fori_loop(0, sections, one, 0)
+
+            else:
+                lax.fori_loop(0, sections, one, 0)
 
     def deliver_table(use, section, device):
         send(tabrow.at[0], tab.at[use, exp], tab_send, tab_recv.at[use], section, device)
@@ -142,6 +162,7 @@
     def drain_table(use, section, device):
         sent(tabrow.at[0], tab_send, section, device)
 
+    tables(deliver_table, True)
     fetch.wait()
 
     def enter(act_on):
@@ -162,14 +183,6 @@
         sent(xin.at[m, y], init_send.at[m, y], sec, device)
 
     enter(send_entering)
-    tables(deliver_table)
-    for copy in weights:
-        copy.start()
-    eout[...] = jnp.zeros_like(eout)
-    for c in range(sections):
-        gain[c : c + 1, :] = jnp.zeros((1, WIDE), F32)
-        gain[c : c + 1, :chunk] = norm_gain[:, c * chunk : (c + 1) * chunk]
-
     spot = iota((1, slots), 1)
     spot_lane = (spot // (half * CAP)) * CAP + lax.rem(spot, CAP)
     spot_block = lax.rem(spot // CAP, half)
@@ -192,8 +205,8 @@
             comb = jnp.where(iota((count, slots), 0).astype(F32) == tok, shares[g], 0.0)
             high = comb.astype(BF16)
             low = (comb - high.astype(F32)).astype(BF16)
-            chi[g] = jnp.concatenate([high, high], axis=1)
-            clo[g] = jnp.concatenate([low, low], axis=1)
+            chi[g] = high
+            clo[g] = low
 
     def prepare_rows(use):
         arrived(tab.at[use], tab_recv.at[use])
@@ -203,6 +216,30 @@
             col = jnp.broadcast_to(tok, (slots, slots)).T[:, :1]
             place[g] = (iota((slots, count), 1).astype(F32) == col).astype(BF16)
 
+    def far_from(x, y):
+        dx = lax.rem(my_x - x + nx, nx)
+        dy = lax.rem(my_y - y + NY, NY)
+        return jnp.minimum(dx, nx - dx) + jnp.minimum(dy, NY - dy) >= FAR
+
+    def rows_to(k, layer, act_on):
+        def one(i, unused):
+            e = lax.rem(i + (my_y + 1) * 2, 2 * NY) + (i // (2 * NY)) * 2 * NY
+            takes = lax.rem(e, 2) == lax.rem(my_y, 2)
+
+            @pl.when(takes | far_from(layer // NZ, lax.rem(e // 2, NY)))
+            def _():
+                act_on(
+                    hrows.at[k, e // GROUP], ein.at[flow, my_chunk],
+                    rows_sem.at[k], ein_sem.at[flow, my_chunk], layer, e,
+                )
+
+            return unused
+
+        lax.fori_loop(0, spread, one, 0)
+
+    def drain_rows(src, dst, send_sem, recv_sem, section, device):
+        sent(src, send_sem, section, device)
+
     def dispatch(source, k, layer):
         for g in range(2):
             x = source[g * half : (g + 1) * half].reshape(count, WIDE)
@@ -211,14 +248,8 @@
                 window, half * CAP, WIDE
             )
 
-        def one(e, unused):
-            send(
-                hrows.at[k, e // GROUP], ein.at[flow, my_chunk],
-                rows_sem.at[k], ein_sem.at[flow, my_chunk], layer, e,
-            )
-            return unused
-
-        lax.fori_loop(0, spread, one, 0)
+        rows_to(k, layer, send)
+
 
     @pl.when(starts)
     def _():
@@ -226,44 +257,85 @@
         arrived(hx.at[first_visit], init_recv)
         dispatch(hx[first_visit], nx, way * last)
 
-    tables(drain_table)
+    tables(deliver_table, False)
+    eout[...] = jnp.zeros_like(eout)
+    eswap[...] = jnp.zeros_like(eswap)
+    for c in range(sections):
+        gain[c : c + 1, :] = jnp.zeros((1, WIDE), F32)
+        gain[c : c + 1, :chunk] = norm_gain[:, c * chunk : (c + 1) * chunk]
+    tables(drain_table, True)
+    tables(drain_table, False)
     enter(sent_entering)
 
     around = sorted(
-        ((dx, dy) for dx in range(nx) for dy in range(NY)),
-        key=lambda o: (min(o[0], nx - o[0]) + min(o[1], NY - o[1]), o),
+        ((dx, dy) for dx in range(nx) for dy in range(NY // 2)),
+        key=lambda o: (min(o[0], nx - o[0]) + 2 * o[1], o),
     )
+    core = lax.rem(exp, 2)
+    sibling = exp + 1 - 2 * core
     columns = sorted(range(nx), key=lambda dx: -min(dx, nx - dx))
 
     def expert_phase(f):
         gate = jnp.zeros((spread * CAP, hid), F32)
         up = jnp.zeros((spread * CAP, hid), F32)
         square = jnp.zeros((spread * CAP, WIDE), F32)
-        for dx, dy in around:
-            c = lax.rem(my_x + dx, nx) * NY + lax.rem(my_y + dy, NY)
-            arrived(ein.at[f, c], ein_sem.at[f, c])
-            x = ein[f, c].astype(F32)
-            square += x * x
-            h = (x * gain[pl.ds(c, 1), :]).astype(BF16)[:, :chunk]
-            rows = pl.ds(pl.multiple_of(c * chunk, 32), chunk)
-            gate += jnp.dot(h, wg[rows, :], preferred_element_type=F32)
-            up += jnp.dot(h, wu[rows, :], preferred_element_type=F32)
+        for passes in (True, False):
+            for dx, half_dy in around:
+                odd = lax.rem(my_y + core, 2) if passes else lax.rem(my_y + core + 1, 2)
+                y = lax.rem(my_y + 2 * half_dy + odd, NY)
+                c = lax.rem(my_x + dx, nx) * NY + y
+                arrived(ein.at[f, c], ein_sem.at[f, c])
+                if passes:
+
+                    @pl.when(jnp.logical_not(far_from(lax.rem(my_x + dx, nx), y)))
+                    def _():
+                        pltpu.make_async_remote_copy(
+                            src_ref=ein.at[f, c], dst_ref=ein.at[f, c],
+                            send_sem=pass_send.at[f], recv_sem=ein_sem.at[f, c],
+                            device_id=(sec, sibling), device_id_type=MESH,
+                        ).start()
+
+                x = ein[f, c].astype(F32)
+                square += x * x
+                h = (x * gain[pl.ds(c, 1), :]).astype(BF16)[:, :chunk]
+                rows = pl.ds(pl.multiple_of(c * chunk, 32), chunk)
+                gate += jnp.dot(h, wg[rows, :], preferred_element_type=F32)
+                up += jnp.dot(h, wu[rows, :], preferred_element_type=F32)
         scale = lax.rsqrt(jnp.sum(square, axis=1, keepdims=True) / width + norm_eps)
         gate = gate * scale
         up = up * scale
         act[...] = (gate / (1.0 + jnp.exp(-gate)) * up).astype(BF16)
-        mine = lax.rem(exp, GROUP) * window + exp // GROUP
-        for dx in columns:
+        for n, dx in enumerate(columns):
             x = lax.rem(my_x + dx, nx)
             cols = pl.ds(pl.multiple_of(x * block, 128), block)
-            part[...] = jnp.dot(act[...], wd[:, cols], preferred_element_type=F32).astype(BF16)
+            part[n] = jnp.dot(act[...], wd[:, cols], preferred_element_type=F32).astype(BF16)
             for y in range(NY):
-                c = x * NY + y
-                eout[f, c, :, :chunk] = part[:, y * chunk : (y + 1) * chunk]
-                send(
-                    eout.at[f, c], hparts.at[my_x, mine], eout_sem.at[f], parts_sem.at[my_x],
-                    x * NZ + my_z, home_of(f, x, y),
-                )
+
+                @pl.when(core != y % 2)
+                def _():
+                    c = x * NY + y
+                    eswap[f, x, y // 2, :, :chunk] = part[n, :, y * chunk : (y + 1) * chunk]
+                    pltpu.make_async_remote_copy(
+                        src_ref=eswap.at[f, x, y // 2], dst_ref=pin.at[f, x, y // 2],
+                        send_sem=swap_send.at[f], recv_sem=pin_sem.at[f, c],
+                        device_id=(sec, sibling), device_id_type=MESH,
+                    ).start()
+
+        for n, dx in enumerate(columns):
+            x = lax.rem(my_x + dx, nx)
+            for y in range(NY):
+
+                @pl.when(core == y % 2)
+                def _():
+                    c = x * NY + y
+                    arrived(pin.at[f, x, y // 2], pin_sem.at[f, c])
+                    own = part[n, :, y * chunk : (y + 1) * chunk].astype(F32)
+                    other = pin[f, x, y // 2, :, :chunk].astype(F32)
+                    eout[f, x, y // 2, :, :chunk] = (own + other).astype(BF16)
+                    send(
+                        eout.at[f, x, y // 2], hparts.at[my_x, exp // GROUP], eout_sem.at[f],
+                        parts_sem.at[my_x], x * NZ + my_z, home_of(f, x, y),
+                    )
 
     def home_phase(k, layer):
         following = layer + 1 - 2 * way
@@ -281,7 +353,7 @@
         arrived(hparts.at[k], parts_sem.at[k])
         for g in range(2):
             got = hparts[k, :, g * half * CAP : (g + 1) * half * CAP, :]
-            got = got.reshape(2 * slots, WIDE)
+            got = got.reshape(slots, WIDE)
             added = jnp.dot(chi[g], got, preferred_element_type=F32)
             added += jnp.dot(clo[g], got, preferred_element_type=F32)
             old = hx[k, g * half : (g + 1) * half].reshape(count, WIDE)
@@ -291,6 +363,7 @@
         @pl.when(onward)
         def _():
             dispatch(hnew[k], k, following)
+
             pltpu.make_async_remote_copy(
                 src_ref=hnew.at[k], dst_ref=hx.at[following // NZ],
                 send_sem=move_send.at[k], recv_sem=move_recv.at[following // NZ],
@@ -334,21 +407,34 @@
     lax.fori_loop(0, sections, step, 0)
 
     for f in range(FLOWS):
-
-        @pl.when(f == flow)
-        def _():
-            arrived(eout.at[f, 1:], eout_sem.at[f])
-
-        @pl.when(f != flow)
-        def _():
-            arrived(eout.at[f], eout_sem.at[f])
+        arrived(eswap.at[f], swap_send.at[f])
+        inner = [
+            (dx, dy) for dx in range(nx) for dy in range(NY)
+            if min(dx, nx - dx) + min(dy, NY - dy) < FAR
+        ]
+        for parity in range(2):
+            passed = sum(1 for _, dy in inner if dy % 2 == parity)
+
+            @pl.when(lax.rem(my_y + core, 2) == parity)
+            def _():
+                arrived(ein.at[f, :passed], pass_send.at[f])
+
+        own = (f == flow) & (core == lax.rem(my_y, 2))
+
+        @pl.when(own)
+        def _():
+            arrived(ein.at[f, 1 : sections // 2], eout_sem.at[f])
+
+        @pl.when(jnp.logical_not(own))
+        def _():
+            arrived(ein.at[f, : sections // 2], eout_sem.at[f])
 
     for k in range(nx):
         final = ends & (k == (1 - way) * (nx - 1))
 
         @pl.when(jnp.logical_not(final))
         def _():
-            arrived(hparts.at[k], rows_sem.at[k])
+            rows_to(k, NZ * k + my_z + 1 - 2 * way, drain_rows)
             arrived(hnew.at[k], move_send.at[k])
 
         @pl.when(final)
@@ -359,9 +445,7 @@
 
     @pl.when(starts)
     def _():
-        lax.fori_loop(
-            0, spread, lambda e, unused: (sent(hrows.at[nx, 0], rows_sem.at[nx], way * last, e), unused)[1], 0
-        )
+        rows_to(nx, way * last, drain_rows)
 
     for f in range(FLOWS):
         arrived(fin.at[f], fin_recv.at[f])
@@ -375,6 +459,7 @@
     chunk = width // sections
     hid = w_gate.shape[2]
     nx = sections // NZ
+    topk = route_ids.shape[4]
     window = spread // GROUP
     rows = spread * CAP
     slots = spread // 2 * CAP * window
@@ -386,7 +471,7 @@
     return pl.pallas_call(
         kernel,
         out_shape=jax.ShapeDtypeStruct((2, 2, tokens, chunk), BF16),
-        in_specs=[hbm, vmem, hbm, hbm, hbm, vmem, vmem],
+        in_specs=[hbm, hbm, hbm, hbm, hbm, hbm, hbm],
         out_specs=vmem,
         scratch_shapes=[
             pltpu.VMEM((width, hid), BF16),
@@ -396,19 +481,29 @@
             pltpu.VMEM((2, NY, tokens, WIDE), BF16),
             pltpu.VMEM((sections, WIDE), F32),
             pltpu.VMEM((FLOWS, sections, rows, WIDE), BF16),
-            pltpu.VMEM((FLOWS, sections, rows, WIDE), BF16),
-            pltpu.VMEM((rows, chunk * NY), BF16),
+            pltpu.VMEM((FLOWS, nx, NY // 2, rows, WIDE), BF16),
+            pltpu.VMEM((nx, rows, chunk * NY), BF16),
             pltpu.VMEM((rows, hid), BF16),
             pltpu.VMEM((nx, spread, tokens, WIDE), BF16),
             pltpu.VMEM((nx, spread, tokens, WIDE), BF16),
             pltpu.VMEM((nx + 1, window, rows, WIDE), BF16),
-            pltpu.VMEM((nx, spread, rows, WIDE), BF16),
+            pltpu.VMEM((nx, window, rows, WIDE), BF16),
             pltpu.VMEM((FLOWS, tokens, WIDE), BF16),
             pltpu.VMEM((1, 1, lanes), F32),
             pltpu.VMEM((2 * nx + 1, spread, 1, lanes), F32),
-            pltpu.VMEM((2, count, 2 * slots), BF16),
-            pltpu.VMEM((2, count, 2 * slots), BF16),
+            pltpu.VMEM((2, count, slots), BF16),
+            pltpu.VMEM((2, count, slots), BF16),
             pltpu.VMEM((2, slots, count), BF16),
+            pltpu.SemaphoreType.REGULAR,
+            pltpu.VMEM((1, width), F32),
+            pltpu.VMEM((2, 2, 1, topk, tokens), jnp.int32),
+            pltpu.VMEM((2, 2, 1, topk, tokens), F32),
+            dma((3,)),
+            pltpu.VMEM((FLOWS, nx, NY // 2, rows, WIDE), BF16),
+            pltpu.VMEM((FLOWS, nx, NY // 2, rows, WIDE), BF16),
+            dma((FLOWS,)),
+            dma((FLOWS, sections)),
+            dma((FLOWS,)),
             dma((3,)),
             dma,
             dma((2, NY)),
@@ -425,7 +520,7 @@
             dma((2 * nx + 1,)),
         ],
         compiler_params=pltpu.CompilerParams(
-            has_side_effects=True, vmem_limit_bytes=48 * 2**20
+            has_side_effects=True, vmem_limit_bytes=60 * 2**20
         ),
         cost_estimate=pl.CostEstimate(
             flops=2 * FLOWS * rows * width * hid * 3,
@@ -433,7 +528,10 @@
             transcendentals=0,
         ),
         name="relay",
-    )(entering, norm_gain, w_gate, w_up, w_down, route_ids, route_scores)
+    )(
+        entering, norm_gain, w_gate, w_up, w_down,
+        jnp.swapaxes(route_ids, 3, 4), jnp.swapaxes(route_scores, 3, 4),
+    )
 
 
 def solution(mesh):

time: 340 us -> 293 us (0.86); the launches traced: 336 us -> 293 us
  Pallas kernels: 330 us -> 292 us
  local copies, waits for them, and re-layouts: 6.15 us -> 1.47 us
    pallas_call x1, Pallas kernels: 330 us -> 292 us  [on_device(): pl.pallas_call(kernel, out_shape=jax.ShapeDtypeStruct((2, 2, tokens, chun...]
    unnamed x9 -> x1, local copies, waits for them, and re-layouts: 6.15 us -> 1.47 us
where the time goes in v3:
time: 293 us
  Pallas kernels  292 us (100%)
    pallas_call x1, Pallas kernels, on_device(): pl.pallas_call(kernel, out_shape=jax.ShapeDtypeStruct((2, 2, tokens, chun...  292 us

profile of v3, /device:TPU:61, one launch (start us, length us, event | category | flops | bytes accessed | tf_op | source)
XLA Modules:
  0.0 293.1 jit_solution(10225135938765181481)
XLA Ops:
  0.0 291.7 %relay.1 = bf16[2,2,32,224]{3,2,1,0:T(8,128)(2,1)} custom-call(bf16[2,2,32,3584]{3,2,1,0:T(8,128)(2,1)} %entering.1, f32[1,3584]{1,0:T(1,128)} %gain_h.1, bf16[1,3584,512]{2,1,0:T(8,128)(2,1)} %wg_h.1, bf16[1,3584,512]{2,1,0:T(8,128)(2,1)} %wu_h.1, bf16[1,512,3584]{2,1,0:T(8,128)(2,1)} %wd_h.1, s32[2,2,1,8,32]{4,3,2,1,0:T(8,128)} %bitcast.2, ...), custom_call_target="tpu_custom_call" | custom-call | flops 1409286144 | bytes 11010048 | tf_op jit(solution)/shard_map/relay/pallas_call | solution.py:471
  291.7 1.5 copy.9

commit v4 on v3

--- a/solution.py
+++ b/solution.py
@@ -32,7 +32,7 @@
     entering, gain_h, wg_h, wu_h, wd_h, ids_h, scores_h, out,
     wg, wu, wd, raw, xin, gain, ein, eout, part, act,
     hx, hnew, hrows, hparts, fin, tabrow, tab, chi, clo, place,
-    turn, norm_gain, ids, scores, gain_sem, eswap, pin, swap_send, pin_sem, pass_send,
+    picked, mhi, mlo, norm_gain, ids, scores, gain_sem, eswap, pin, swap_send, pin_sem, pass_send,
     w_sem, raw_sem, init_send, init_recv, ein_sem, eout_sem, rows_sem, parts_sem,
     move_send, move_recv, fin_send, fin_recv, tab_send, tab_recv,
 ):
@@ -216,6 +216,11 @@
             col = jnp.broadcast_to(tok, (slots, slots)).T[:, :1]
             place[g] = (iota((slots, count), 1).astype(F32) == col).astype(BF16)
 
+    def pick_rows(k):
+        for g in range(2):
+            x = hx[k, g * half : (g + 1) * half].reshape(count, WIDE)
+            picked[g] = jnp.dot(place[g], x, preferred_element_type=F32)
+
     def far_from(x, y):
         dx = lax.rem(my_x - x + nx, nx)
         dy = lax.rem(my_y - y + NY, NY)
@@ -240,10 +245,17 @@
     def drain_rows(src, dst, send_sem, recv_sem, section, device):
         sent(src, send_sem, section, device)
 
-    def dispatch(source, k, layer):
+    def sums(k, g, high, low):
+        got = hparts[k, :, g * half * CAP : (g + 1) * half * CAP, :].reshape(slots, WIDE)
+        added = jnp.dot(high, got, preferred_element_type=F32)
+        return added + jnp.dot(low, got, preferred_element_type=F32)
+
+    def dispatch(k, layer, added):
         for g in range(2):
-            x = source[g * half : (g + 1) * half].reshape(count, WIDE)
-            rows = jnp.dot(place[g], x, preferred_element_type=F32).astype(BF16)
+            rows = picked[g]
+            if added:
+                rows += sums(added[0], g, mhi[g], mlo[g])
+            rows = rows.astype(BF16)
             hrows[k, :, g * half * CAP : (g + 1) * half * CAP, :] = rows.reshape(
                 window, half * CAP, WIDE
             )
@@ -255,7 +267,8 @@
     def _():
         prepare_rows(2 * nx)
         arrived(hx.at[first_visit], init_recv)
-        dispatch(hx[first_visit], nx, way * last)
+        pick_rows(first_visit)
+        dispatch(nx, way * last, ())
 
     tables(deliver_table, False)
     eout[...] = jnp.zeros_like(eout)
@@ -273,7 +286,7 @@
     )
     core = lax.rem(exp, 2)
     sibling = exp + 1 - 2 * core
-    columns = sorted(range(nx), key=lambda dx: -min(dx, nx - dx))
+    columns = [dx for dx in (1, 2, 3, 0) if dx < nx]
 
     def expert_phase(f):
         gate = jnp.zeros((spread * CAP, hid), F32)
@@ -345,25 +358,31 @@
         @pl.when(onward)
         def _():
             prepare_rows(nx + k)
+            for g in range(2):
+                mhi[g] = jnp.dot(place[g], chi[g], preferred_element_type=F32).astype(BF16)
+                mlo[g] = jnp.dot(place[g], clo[g], preferred_element_type=F32).astype(BF16)
 
         @pl.when(jnp.logical_not(starts & (k == first_visit)))
         def _():
             arrived(hx.at[k], move_recv.at[k])
 
+        @pl.when(onward)
+        def _():
+            pick_rows(k)
+
         arrived(hparts.at[k], parts_sem.at[k])
+
+        @pl.when(onward)
+        def _():
+            dispatch(k, following, (k,))
+
         for g in range(2):
-            got = hparts[k, :, g * half * CAP : (g + 1) * half * CAP, :]
-            got = got.reshape(slots, WIDE)
-            added = jnp.dot(chi[g], got, preferred_element_type=F32)
-            added += jnp.dot(clo[g], got, preferred_element_type=F32)
             old = hx[k, g * half : (g + 1) * half].reshape(count, WIDE)
-            new = (old.astype(F32) + added).astype(BF16)
+            new = (old.astype(F32) + sums(k, g, chi[g], clo[g])).astype(BF16)
             hnew[k, g * half : (g + 1) * half] = new.reshape(half, tokens, WIDE)
 
         @pl.when(onward)
         def _():
-            dispatch(hnew[k], k, following)
-
             pltpu.make_async_remote_copy(
                 src_ref=hnew.at[k], dst_ref=hx.at[following // NZ],
                 send_sem=move_send.at[k], recv_sem=move_recv.at[following // NZ],
@@ -494,7 +513,9 @@
             pltpu.VMEM((2, count, slots), BF16),
             pltpu.VMEM((2, count, slots), BF16),
             pltpu.VMEM((2, slots, count), BF16),
-            pltpu.SemaphoreType.REGULAR,
+            pltpu.VMEM((2, slots, WIDE), F32),
+            pltpu.VMEM((2, slots, slots), BF16),
+            pltpu.VMEM((2, slots, slots), BF16),
             pltpu.VMEM((1, width), F32),
             pltpu.VMEM((2, 2, 1, topk, tokens), jnp.int32),
             pltpu.VMEM((2, 2, 1, topk, tokens), F32),

time: 293 us -> 292 us (level)
  no operation moved by 1% of the time
where the time goes in v4:
time: 292 us; the launch traced here: 291 us
  Pallas kernels  290 us (99%)
    pallas_call x1, Pallas kernels, on_device(): pl.pallas_call(kernel, out_shape=jax.ShapeDtypeStruct((2, 2, tokens, chun...  290 us

profile of v4, /device:TPU:61, one launch (start us, length us, event | category | flops | bytes accessed | tf_op | source)
XLA Modules:
  0.0 291.3 jit_solution(17667908778423413347)
XLA Ops:
  0.0 289.9 %relay.1 = bf16[2,2,32,224]{3,2,1,0:T(8,128)(2,1)} custom-call(bf16[2,2,32,3584]{3,2,1,0:T(8,128)(2,1)} %entering.1, f32[1,3584]{1,0:T(1,128)} %gain_h.1, bf16[1,3584,512]{2,1,0:T(8,128)(2,1)} %wg_h.1, bf16[1,3584,512]{2,1,0:T(8,128)(2,1)} %wu_h.1, bf16[1,512,3584]{2,1,0:T(8,128)(2,1)} %wd_h.1, s32[2,2,1,8,32]{4,3,2,1,0:T(8,128)} %bitcast.2, ...), custom_call_target="tpu_custom_call" | custom-call | flops 1409286144 | bytes 11010048 | tf_op jit(solution)/shard_map/relay/pallas_call | solution.py:490
  289.9 1.5 copy.9

commit v5 on v4

--- a/solution.py
+++ b/solution.py
@@ -228,7 +228,7 @@
 
     def rows_to(k, layer, act_on):
         def one(i, unused):
-            e = lax.rem(i + (my_y + 1) * 2, 2 * NY) + (i // (2 * NY)) * 2 * NY
+            e = lax.rem(i + (my_y + 1) * 2, 2 * NY) + lax.rem(i // (2 * NY) + 1 + way, 2) * 2 * NY
             takes = lax.rem(e, 2) == lax.rem(my_y, 2)
 
             @pl.when(takes | far_from(layer // NZ, lax.rem(e // 2, NY)))

time: 292 us -> 288 us (0.986)
  Pallas kernels: 290 us -> 284 us
    pallas_call x1, Pallas kernels: 290 us -> 284 us  [on_device(): pl.pallas_call(kernel, out_shape=jax.ShapeDtypeStruct((2, 2, tokens, chun...]
where the time goes in v5:
time: 288 us; the launch traced here: 285 us
  Pallas kernels  284 us (99%)
    pallas_call x1, Pallas kernels, on_device(): pl.pallas_call(kernel, out_shape=jax.ShapeDtypeStruct((2, 2, tokens, chun...  284 us

profile of v5, /device:TPU:61, one launch (start us, length us, event | category | flops | bytes accessed | tf_op | source)
XLA Modules:
  0.0 285.2 jit_solution(15887716318634690565)
XLA Ops:
  0.0 283.7 %relay.1 = bf16[2,2,32,224]{3,2,1,0:T(8,128)(2,1)} custom-call(bf16[2,2,32,3584]{3,2,1,0:T(8,128)(2,1)} %entering.1, f32[1,3584]{1,0:T(1,128)} %gain_h.1, bf16[1,3584,512]{2,1,0:T(8,128)(2,1)} %wg_h.1, bf16[1,3584,512]{2,1,0:T(8,128)(2,1)} %wu_h.1, bf16[1,512,3584]{2,1,0:T(8,128)(2,1)} %wd_h.1, s32[2,2,1,8,32]{4,3,2,1,0:T(8,128)} %bitcast.2, ...), custom_call_target="tpu_custom_call" | custom-call | flops 1409286144 | bytes 11010048 | tf_op jit(solution)/shard_map/relay/pallas_call | solution.py:490
  283.7 1.5 copy.9
